TPU v7x, 32 devices: a whole 2x2x4 slice. The times are simulated.
32 devices in a mesh: batch: 2 (over y), freq: 8 (over z, x), elem: 2 (over core).
Axes of the slice: x: 2, y: 2, z: 4, core: 2. Of those that a mesh axis runs over, the one named last changes fastest.
Arguments:
- flaw_cells: int32 [512], P('batch'), parts along dimension 0, may hold values from 0 to 255, each once
- flaw_blocks: int32 [16], P('batch'), parts along dimension 0, may hold values from 0 to 7, each once
- element_channel: int32 [256], P('elem'), may hold values from 0 to 255, each once
- focal_delay: float32 [256, 256], replicated, may hold values from 0 to 64
- beam_field: bfloat16 [128, 2, 256, 256], P('freq', None, 'elem'), may hold values from -0.125 to 0.125
- flaw_size: float32 [4, 128], P('batch'), parts along dimension 0, may hold values from 0.5 to 4
- flaw_slope: float32 [4, 128], P('batch'), parts along dimension 0, may hold values from 0.2 to 1
- noise_level: float32 [4, 128], P(('batch', 'elem'), 'freq'), parts along dimension 0, may hold values from 0.5 to 5
Outputs:
- flaw_peak: float32 [4, 128], P(('batch', 'elem'), 'freq'), parts along dimension 0
- detection: float32 [4, 128], P(('batch', 'elem'), 'freq'), parts along dimension 0
There are 2 independent parts, one for each index of `batch`. A program takes and returns all parts, laid end to end along the dimension named above; an argument that names none is the same for every part. Nothing has to cross between parts.
Inputs may be any that keep to these rules, and one draw needn't show every extreme that they name: `flaw_cells`: every site holds exactly one flaw. `flaw_blocks`: every scan block belongs to exactly one flaw group. `element_channel`: every channel drives exactly one element.
All inputs are finite; a program needn't handle non-finite values.
Results may differ from a plain program's by a relative error of at most 0.0011.
Values may be sent and summed in bfloat16 or wider, within the bound.
No kernel may reach another device: no remote copies, remote signals or barrier semaphores. Data moves between devices by JAX's collectives and lax.ppermute only.
A program may use at most 64 MiB of HBM per device.

v0:
```python
import functools
import math

import jax
import jax.numpy as jnp
from jax import lax
from jax.experimental import pallas as pl
from jax.experimental.pallas import tpu as pltpu
from jax.sharding import PartitionSpec as P

W_DEV = 16
W_HALF = W_DEV // 2
FG = 128
NB = 4
SB = 32
T_CAP = 1024

EDGE = 0.6
STEEP = 3.0
EPS = 1e-05

ROWS = NB * SB
VMEM_BYTES = 48 * 1024 * 1024


def sin_half_turn(turns):
    angle = turns * math.pi
    square = angle * angle
    sine = 1.0 / 6227020800.0
    for factorial in (-39916800.0, 362880.0, -5040.0, 120.0, -6.0, 1.0):
        sine = sine * square + 1.0 / factorial
    cosine = 1.0 / 479001600.0
    for factorial in (-3628800.0, 40320.0, -720.0, 24.0, -2.0, 1.0):
        cosine = cosine * square + 1.0 / factorial
    return sine * angle, cosine


def sincos_turns(turns):
    rest = turns - jnp.floor(turns + 0.5)
    sine, cosine = sin_half_turn(rest)
    return 2.0 * sine * cosine, 1.0 - 2.0 * sine * sine


def dot(left, right, contract):
    return lax.dot_general(
        left, right, (contract, ((), ())), preferred_element_type=jnp.float32
    )


def slot_masks(slots):
    half = slots // 2
    between = (2, half, half + 1, 3, slots - 1)
    return (0, 1, *between, slots - 2), (0, slots - 2, *between, 1)


def partner(slots, slot):
    index = lax.axis_index("freq")
    inner = ((index * 2) ^ index) & (slots // 2) != 0
    outer_masks, inner_masks = slot_masks(slots)
    mask = jnp.zeros_like(slot)
    for s in range(1, slots):
        mask = jnp.where(slot == s, jnp.where(inner, inner_masks[s], outer_masks[s]), mask)
    return mask ^ index


def slot_order(slots):
    size = FG // slots
    row = lax.broadcasted_iota(jnp.int32, (FG, 1), 0)
    column = lax.broadcasted_iota(jnp.int32, (FG, FG), 1)
    if slots > 1:
        row = partner(slots, row // size) * size + row % size
    return row == column


def flaw_pick(slots, which, cells_ref):
    cells = jnp.where(which == 0, cells_ref[:, :FG], cells_ref[:, FG:])
    cell_sel = lax.broadcasted_iota(jnp.int32, (cells_ref.shape[1], FG), 0) == cells
    return dot(
        slot_order(slots).astype(jnp.bfloat16), cell_sel.astype(jnp.bfloat16), ((1,), (1,))
    ).astype(jnp.bfloat16)


def delays_of(channel_ref, delay_ref, blocks_ref, groups, elements):
    lane = lax.broadcasted_iota(jnp.int32, (1, 2 * ROWS), 1)
    position = lane & (SB - 1)
    for j in range(2 * NB):
        block = blocks_ref[groups[j // NB] * NB + j % NB]
        position = position + jnp.where((lane >> 5) == j, block * SB, 0)
    channels, positions = delay_ref.shape
    scan_sel = (
        lax.broadcasted_iota(jnp.int32, (positions, 2 * ROWS), 0) == position
    ).astype(jnp.bfloat16)
    channel_sel = (
        (lax.broadcasted_iota(jnp.int32, (channels, elements), 0) == channel_ref[...])
        .astype(jnp.float32)
        .T.astype(jnp.bfloat16)
    )
    rest = delay_ref[...]
    pieces = []
    for _ in range(3):
        pieces.append(rest.astype(jnp.bfloat16))
        rest = rest - pieces[-1].astype(jnp.float32)
    moved = dot(jnp.concatenate(pieces, axis=0), scan_sel, ((1,), (0,))).astype(jnp.bfloat16)
    delays = None
    for i in range(3):
        piece = dot(channel_sel, moved[i * channels : (i + 1) * channels], ((1,), (0,)))
        delays = piece if delays is None else delays + piece
    return delays


def turned(law, step):
    return law[0] * step[0] - law[1] * step[1], law[1] * step[0] + law[0] * step[1]


def focal_base(freq_total, delays):
    first_freq = lax.axis_index("freq") * W_DEV
    phase = delays * (0.5 / freq_total)
    unit = sincos_turns(phase)[::-1]
    base = sincos_turns(phase * first_freq.astype(jnp.float32))[::-1]
    return base, turned(unit, unit), turned(base, unit)


def kirchhoff(freq_total, slots, which, size_ref, slope_ref):
    first_freq = lax.axis_index("freq") * W_DEV
    order = slot_order(slots)
    size = size_ref[pl.ds(which, 1), :]
    turn = size * slope_ref[pl.ds(which, 1), :] * (1.0 / freq_total)
    size = jnp.sum(jnp.where(order, size, 0.0), axis=1, keepdims=True)
    turn = jnp.sum(jnp.where(order, turn, 0.0), axis=1, keepdims=True)
    freq = first_freq + lax.broadcasted_iota(jnp.int32, (FG, FG), 1)
    sine, cosine = sincos_turns(turn * freq.astype(jnp.float32))
    return size * (1.0 + EDGE) * cosine, size * (EDGE - 1.0) * sine


def store_law(law_ref, law, step):
    elements = law_ref.shape[1] // 2
    for w in range(W_HALF):
        c = law[0].astype(jnp.bfloat16)
        s = law[1].astype(jnp.bfloat16)
        law_ref[w, :elements, :ROWS] = c
        law_ref[w, :elements, ROWS:] = -s
        law_ref[w, elements:, :ROWS] = s
        law_ref[w, elements:, ROWS:] = c
        if w < W_HALF - 1:
            law = turned(law, step)


def pick_fields(parity, picks, field_ref, wait, picked_refs):
    elements, sites = field_ref.shape[3:]
    for w in range(W_HALF):
        wait(w)
        picked = dot(
            picks, field_ref[w, parity].reshape(2 * elements, sites), ((1,), (1,))
        ).astype(jnp.bfloat16)
        for i, ref in enumerate(picked_refs):
            ref[w] = picked[i * FG : (i + 1) * FG]


def store_spectra(parity, picked_ref, law_ref, k_real, k_imag, out_ref, first):
    for w in range(W_HALF):
        product = dot(picked_ref[w], law_ref[w], ((1,), (0,)))
        real_part = product[:, :ROWS]
        imag_part = product[:, ROWS:]
        kr = k_real[:, 2 * w + parity : 2 * w + parity + 1]
        ki = k_imag[:, 2 * w + parity : 2 * w + parity + 1]
        out_ref[first + 2 * w] = (kr * real_part - ki * imag_part).astype(jnp.bfloat16)
        out_ref[first + 2 * w + 1] = (kr * imag_part + ki * real_part).astype(jnp.bfloat16)


def other_even_kernel(freq_total, slots, *refs):
    field_hbm, *small_hbm = refs[:7]
    out_ref, own_picked_ref, field_ref, *kept = refs[7:25]
    small, (field_sem, small_sem, *scratch) = refs[25:31], refs[31:]
    delay_ref, channel_ref, blocks_ref, cells_ref, size_ref, slope_ref = small
    picked_ref, law_ref = scratch
    copies = [
        pltpu.make_async_copy(source, target, small_sem.at[i])
        for i, (source, target) in enumerate(zip(small_hbm, small))
    ]
    for copy in copies:
        copy.start()
    part = W_HALF // 2
    field_copies = [
        pltpu.make_async_copy(
            field_hbm.at[pl.ds(i * part, part), parity],
            field_ref.at[pl.ds(i * part, part), parity],
            field_sem.at[parity, i],
        )
        for parity in range(2)
        for i in range(2)
    ]
    for copy in field_copies:
        copy.start()
    for copy in copies:
        copy.wait()
    group = lax.axis_index("elem")
    groups = (1 - group, group)
    picks = jnp.concatenate(
        [flaw_pick(slots, which, cells_ref) for which in groups], axis=0
    )
    factors = [
        kirchhoff(freq_total, slots, which, size_ref, slope_ref) for which in groups
    ]
    delays = delays_of(channel_ref, delay_ref, blocks_ref, groups, field_ref.shape[3])
    laws = [
        focal_base(freq_total, delays[:, i * ROWS : (i + 1) * ROWS]) for i in range(2)
    ]
    values = [picks]
    for (even, step, odd), factor in zip(laws, factors):
        values += [*even, *step, *odd, *factor]
    for ref, value in zip(kept, [*values[:1], *values[3:]]):
        ref[...] = value
    even, step, _ = laws[0]
    store_law(law_ref, even, step)

    def wait(w):
        if w % part == 0:
            field_copies[w // part].wait()

    pick_fields(0, picks, field_ref, wait, (picked_ref, own_picked_ref))
    store_spectra(0, picked_ref, law_ref, *factors[0], out_ref, 0)
    for copy in field_copies[2:]:
        copy.wait()


def other_odd_kernel(field_ref, picks_ref, *refs):
    step, odd, k_refs = refs[:2], refs[2:4], refs[4:6]
    out_ref, own_picked_ref, picked_ref, law_ref = refs[6:]
    store_law(law_ref, [ref[...] for ref in odd], [ref[...] for ref in step])
    pick_fields(
        1, picks_ref[...], field_ref, lambda w: None, (picked_ref, own_picked_ref)
    )
    store_spectra(1, picked_ref, law_ref, *k_refs, out_ref, 0)


def own_kernel(*refs):
    picked_refs, refs = refs[:2], refs[2:]
    even, step, odd, k_refs = (refs[2 * i : 2 * i + 2] for i in range(4))
    out_ref, law_ref = refs[8:]
    step = [ref[...] for ref in step]
    for parity, law in enumerate((even, odd)):
        store_law(law_ref.at[parity], [ref[...] for ref in law], step)
    for parity in range(2):
        store_spectra(
            parity, picked_refs[parity], law_ref.at[parity], *k_refs, out_ref, parity * W_DEV
        )


def call(kernel, name, in_specs, out_shape, scratch):
    vmem = pl.BlockSpec(memory_space=pltpu.VMEM)
    return pl.pallas_call(
        kernel,
        in_specs=in_specs,
        out_specs=[vmem] * len(out_shape),
        out_shape=out_shape,
        scratch_shapes=scratch,
        compiler_params=pltpu.CompilerParams(vmem_limit_bytes=VMEM_BYTES),
        cost_estimate=pl.CostEstimate(flops=1000, bytes_accessed=1000, transcendentals=0),
        name=name,
    )


def partials(field, small, swap, freq_total, slots):
    elements, sites = field.shape[3:]
    vmem = pl.BlockSpec(memory_space=pltpu.VMEM)
    hbm = pl.BlockSpec(memory_space=pltpu.HBM)
    pinned = [pltpu.with_memory_space_constraint(a, pltpu.HBM) for a in (field, *small)]
    out = jax.ShapeDtypeStruct((W_DEV, FG, ROWS), jnp.bfloat16)
    picked = jax.ShapeDtypeStruct((W_HALF, FG, 2 * elements), jnp.bfloat16)
    law = (W_HALF, 2 * elements, 2 * ROWS)
    base = [jax.ShapeDtypeStruct((elements, ROWS), jnp.float32)] * 2
    factors = [jax.ShapeDtypeStruct((FG, FG), jnp.float32)] * 2
    kept = [jax.ShapeDtypeStruct((2 * FG, sites), jnp.bfloat16)]
    kept += [*base, *base, *factors, *base, *base, *base, *factors]
    work = [pltpu.VMEM(picked.shape, picked.dtype), pltpu.VMEM(law, jnp.bfloat16)]
    even, even_picked, field, picks, *kept = call(
        functools.partial(other_even_kernel, freq_total, slots),
        "other_even",
        [hbm] * len(pinned),
        [out, picked, jax.ShapeDtypeStruct(field.shape, field.dtype), *kept],
        [
            pltpu.SMEM(a.shape, a.dtype) if a.ndim == 1 else pltpu.VMEM(a.shape, a.dtype)
            for a in small
        ]
        + [pltpu.SemaphoreType.DMA((2, 2)), pltpu.SemaphoreType.DMA((len(small),)), *work],
    )(*pinned)
    even = lax.ppermute(even, "elem", swap)
    odd, odd_picked = call(
        other_odd_kernel, "other_odd", [vmem] * 8, [out, picked], work
    )(field, picks, *kept[:6])
    odd = lax.ppermute(odd, "elem", swap)
    (own,) = call(
        own_kernel,
        "own",
        [vmem] * 10,
        [jax.ShapeDtypeStruct((2 * W_DEV, FG, ROWS), jnp.bfloat16)],
        [pltpu.VMEM((2, *law), jnp.bfloat16)],
    )(even_picked, odd_picked, *kept[6:])
    return own, even, odd


def total(own_ref, moved_ref, parity, rows):
    own = own_ref[parity * W_DEV : (parity + 1) * W_DEV, rows]
    both = own.astype(jnp.float32) + moved_ref[:, rows].astype(jnp.float32)
    return jnp.swapaxes(both, 0, 1).astype(jnp.bfloat16)


def add_even_kernel(size, own_ref, even_ref, held_ref):
    for first in range(0, held_ref.shape[0], size):
        rows = pl.ds(first, size)
        held_ref[rows] = total(own_ref, even_ref, 0, rows)


def add_odd_kernel(own_ref, odd_ref, held_ref, *refs):
    size = refs[0].shape[0]
    for slot, ref in enumerate(refs):
        rows = pl.ds(slot * size, size)
        ref[:, :W_DEV] = held_ref[rows]
        ref[:, W_DEV:] = total(own_ref, odd_ref, 1, rows)


def add(own, even, odd, slots):
    vmem = pl.BlockSpec(memory_space=pltpu.VMEM)
    planes, flaws, rows = own.shape
    size = flaws // slots
    shape = jax.ShapeDtypeStruct((flaws, planes // 2, rows), own.dtype)
    kernel = functools.partial(add_even_kernel, min(size, 16))
    (held,) = call(kernel, "add_even", [vmem] * 2, [shape], [])(own, even)
    shapes = [jax.ShapeDtypeStruct((size, planes, rows), own.dtype)] * slots
    return call(add_odd_kernel, "add_odd", [vmem] * 3, shapes, [])(own, odd, held)


def table_kernel(freq_total, slots, table_ref):
    height, depth = table_ref.shape[2:]
    time_block = height // 2
    row = lax.broadcasted_iota(jnp.int32, (height, depth // 2), 0)
    column = lax.broadcasted_iota(jnp.int32, (height, depth // 2), 1)
    out_imag = (row >= time_block).astype(jnp.int32)
    time = pl.program_id(0) * time_block + row - out_imag * time_block
    for parity in range(2):
        freq = (column >> 1) * 2 + parity
        if slots > 1:
            lane = lax.broadcasted_iota(jnp.int32, (1, depth // 2), 1)
            lane = (lane >> 1) * 2 + parity
            freq = partner(slots, lane // W_DEV) * W_DEV + lane % W_DEV
        steps = freq * time + ((column & 1) - out_imag) * (freq_total // 2)
        steps = (steps + 2 * freq_total) & (2 * freq_total - 1)
        _, value = sincos_turns(steps.astype(jnp.float32) * (0.5 / freq_total))
        high = value.astype(jnp.bfloat16)
        table_ref[0, parity, :, : depth // 2] = high
        table_ref[0, parity, :, depth // 2 :] = (
            value - high.astype(jnp.float32)
        ).astype(jnp.bfloat16)


def table(freq_total, slots, times, time_block):
    blocks = times // time_block
    shape = (blocks, 2, 2 * time_block, 2 * freq_total)
    return pl.pallas_call(
        functools.partial(table_kernel, freq_total, slots),
        grid=(blocks,),
        out_specs=pl.BlockSpec((1, *shape[1:]), lambda i: (i, 0, 0, 0)),
        out_shape=jax.ShapeDtypeStruct(shape, jnp.bfloat16),
        compiler_params=pltpu.CompilerParams(vmem_limit_bytes=VMEM_BYTES),
        name="table",
    )()


def peak_kernel(freq_total, folded, sources, *refs):
    count = len(refs) - 5
    table_ref, noise_ref, peak_ref, found_ref, best_ref = refs[count:]
    step = pl.program_id(0)
    columns = peak_ref.shape[1]
    time_block = table_ref.shape[2] // 2

    @pl.when(step == 0)
    def _():
        best_ref[...] = jnp.zeros_like(best_ref)

    width = min(2, columns)
    for first in range(0, columns, width):
        parts = []
        for parity in range(2):
            planes = slice(parity * W_DEV, (parity + 1) * W_DEV)
            spectra = jnp.concatenate(
                [
                    jnp.concatenate(
                        [
                            refs[i][row + first + k, planes, :]
                            for i, row in sources
                        ]
                        * 2,
                        axis=0,
                    )
                    for k in range(width)
                ],
                axis=1,
            )
            parts.append(dot(table_ref[0, parity], spectra, ((1,), (0,))))
        powers = []
        for signal in [parts[0] + parts[1]] + [parts[0] - parts[1]] * folded:
            real_part = signal[:time_block]
            imag_part = signal[time_block:]
            powers.append(real_part * real_part + imag_part * imag_part)
        power = jnp.maximum(powers[0], powers[-1]) if folded else powers[0]
        power = jnp.max(power, axis=0, keepdims=True)
        for k in range(width):
            row = pl.ds(first + k, 1)
            best_ref[row, :] = jnp.maximum(
                best_ref[row, :], power[:, k * ROWS : (k + 1) * ROWS]
            )

    @pl.when(step == pl.num_programs(0) - 1)
    def _():
        largest = jnp.max(best_ref[...], axis=1, keepdims=True)
        shape = best_ref.shape
        diagonal = lax.broadcasted_iota(jnp.int32, shape, 0) == lax.broadcasted_iota(
            jnp.int32, shape, 1
        )
        largest = jnp.max(jnp.where(diagonal, largest, 0.0), axis=0, keepdims=True)
        peak = jnp.sqrt(largest[:, :columns]) * (1.0 / math.sqrt(freq_total))
        score = STEEP * (jnp.log(peak + EPS) - jnp.log(noise_ref[...]))
        peak_ref[...] = peak
        found_ref[...] = 1.0 / (1.0 + jnp.exp(-score))


def peaks(spectra, sources, twiddles, noise_level, freq_total, folded):
    columns = noise_level.shape[1]
    out_spec = pl.BlockSpec((1, columns), lambda i: (0, 0))
    return pl.pallas_call(
        functools.partial(peak_kernel, freq_total, folded, sources),
        grid=(twiddles.shape[0],),
        in_specs=[pl.BlockSpec(a.shape, lambda i: (0, 0, 0)) for a in spectra]
        + [pl.BlockSpec((1, *twiddles.shape[1:]), lambda i: (i, 0, 0, 0)), out_spec],
        out_specs=[out_spec, out_spec],
        out_shape=[jax.ShapeDtypeStruct((1, columns), jnp.float32)] * 2,
        scratch_shapes=[pltpu.VMEM((max(8, columns), ROWS), jnp.float32)],
        compiler_params=pltpu.CompilerParams(vmem_limit_bytes=VMEM_BYTES),
        name="peaks",
    )(*spectra, twiddles, noise_level)


def body(
    flaw_cells,
    flaw_blocks,
    element_channel,
    focal_delay,
    beam_field,
    flaw_size,
    flaw_slope,
    noise_level,
):
    freq_count = lax.axis_size("freq")
    freq_total = W_DEV * freq_count
    sample_count = min(T_CAP, 2 * freq_total)
    swap = [(0, 1), (1, 0)]
    direct = freq_count == 8
    slots = freq_count if direct else 1
    small = (
        focal_delay,
        element_channel.reshape(1, -1),
        flaw_blocks,
        flaw_cells.reshape(1, -1),
        flaw_size,
        flaw_slope,
    )
    folded = sample_count == 2 * freq_total
    times = sample_count // 2 if folded else sample_count
    twiddles = table(freq_total, slots, times, min(128, times))
    field = beam_field.reshape(W_HALF, 2, *beam_field.shape[1:])
    parts = add(*partials(field, small, swap, freq_total, slots), slots)
    if direct:
        half = slots // 2
        spectra = []
        for slot, masks in enumerate(zip(*slot_masks(slots))):
            pairs = [(a, a ^ masks[((2 * a) ^ a) & half != 0]) for a in range(slots)]
            spectra.append(lax.ppermute(parts[slot], "freq", pairs) if slot else parts[slot])
        spectra = [*spectra[1:], spectra[0]]
        sources = [((slot - 1) % slots, 0) for slot in range(slots)]
    else:
        spectra = [
            lax.all_to_all(parts[0], "freq", split_axis=0, concat_axis=0, tiled=True)
        ]
        sources = [(0, s * (FG // freq_count)) for s in range(freq_count)]
    return tuple(peaks(spectra, sources, twiddles, noise_level, freq_total, folded))


def solution(mesh):
    in_specs = (
        P("batch"),
        P("batch"),
        P("elem"),
        P(),
        P("freq", None, "elem", None),
        P("batch", None),
        P("batch", None),
        P(("batch", "elem"), "freq"),
    )
    out_specs = (P(("batch", "elem"), "freq"), P(("batch", "elem"), "freq"))
    return jax.shard_map(body, mesh=mesh, in_specs=in_specs, out_specs=out_specs, check_vma=False)
```

profile of v0, /device:TPU:0, one launch (start us, length us, event | category | flops | bytes accessed | tf_op | source)
XLA Modules:
  0.0 35.3 jit_solution(6457872437138371167)
XLA Ops:
  0.6 3.4 %other_even.1 = (bf16[16,128,128]{2,1,0:T(8,128)(2,1)S(1)}, bf16[8,128,256]{2,1,0:T(8,128)(2,1)S(1)}, bf16[8,2,2,128,256]{4,3,2,1,0:T(8,128)(2,1)S(1)}, bf16[256...) custom-call(bf16[8,2,2,128,256]{4,3,2,1,0:T(8,128)(2,1)} %bitcast.3,, ...), custom_call_target="tpu_custom_call" | custom-call | flops 1000 | bytes 1000 | tf_op jit(solution)/shard_map/other_even/pallas_call | solution.py:276
  4.0 0.5 %collective-permute-start.1 = (bf16[16,128,128]{2,1,0:T(8,128)(2,1)S(1)}, bf16[16,128,128]{2,1,0:T(8,128)(2,1)S(1)}, u32[]{:S(2)}, u32[]{:S(2)}) collective-permute-start(bf16[16,128,128]{2,1,0:T(8,128)(2,1)S(1)} %get-tuple-element.49), channel_id=1, source_target_pairs={{0,1},{1,0},{2,3},{3,2},{4,5},{5,4},{6,7},{7,6},{8,9},{9,8},{10,11... | collective-permute-start | bytes 1572872 | tf_op jit(solution)/shard_map/ppermute | solution.py:287
  4.5 0.7 %other_odd.1 = (bf16[16,128,128]{2,1,0:T(8,128)(2,1)S(1)}, bf16[8,128,256]{2,1,0:T(8,128)(2,1)S(1)}) custom-call(bf16[8,2,2,128,256]{4,3,2,1,0:T(8,128)(2,1)S(1)} %get-tuple-element.31.field_ref, bf16[256,256]{1,0:T(8,128)(2,1)S(1)} %get-tuple-element.32.picks_ref, f32[128,128]{1,0:T(8,128)S(1)} %get-tuple-element.33.refs_0_, ...), custom_call_target="tpu_custom_call" | custom-call | flops 1000 | bytes 1000 | tf_op jit(solution)/shard_map/other_odd/pallas_call | solution.py:288
  5.3 0.1 collective-permute-start
  5.4 1.0 %own.1.own_ref = bf16[32,128,128]{2,1,0:T(8,128)(2,1)S(1)} custom-call(bf16[8,128,256]{2,1,0:T(8,128)(2,1)S(1)} %get-tuple-element.30.refs_0_, bf16[8,128,256]{2,1,0:T(8,128)(2,1)S(1)} %get-tuple-element.39.refs_1_, f32[128,128]{1,0:T(8,128)S(1)} %get-tuple-element.40.refs_2_, f32[128,128]{1,0:T(8,128)S(1)} %get-tuple-element.41.refs_3_, ...), custom_call_target="tpu_custom_call" | custom-call | flops 1000 | bytes 1000 | tf_op jit(solution)/shard_map/own/pallas_call | solution.py:292
  6.4 0.0 copy-start
  6.4 0.0 collective-permute-done.1.even_ref
  6.4 0.3 add_even.1.held_ref
  6.7 0.5 %collective-permute-done.odd_ref = bf16[16,128,128]{2,1,0:T(8,128)(2,1)S(1)} collective-permute-done((bf16[16,128,128]{2,1,0:T(8,128)(2,1)S(1)}, bf16[16,128,128]{2,1,0:T(8,128)(2,1)S(1)}, u32[]{:S(2)}, u32[]{:S(2)}) %collective-permute-start) | collective-permute-done | bytes 524320 | tf_op jit(solution)/shard_map/ppermute | solution.py:291
  7.2 0.3 add_odd.1
  7.6 2.7 %collective-permute-start.2 = (bf16[16,32,128]{2,1,0:T(8,128)(2,1)S(1)}, bf16[16,32,128]{2,1,0:T(8,128)(2,1)S(1)}, u32[]{:S(2)}, u32[]{:S(2)}) collective-permute-start(bf16[16,32,128]{2,1,0:T(8,128)(2,1)S(1)} %get-tuple-element.50), channel_id=1, source_target_pairs={{0,2},{2,0},{4,8},{6,10},{8,4},{10,6},{12,14},{14,12},{1,3},{3,1},... | collective-permute-start | bytes 393224 | tf_op jit(solution)/shard_map/ppermute | solution.py:477
  10.3 1.7 %collective-permute-start.3 = (bf16[16,32,128]{2,1,0:T(8,128)(2,1)S(1)}, bf16[16,32,128]{2,1,0:T(8,128)(2,1)S(1)}, u32[]{:S(2)}, u32[]{:S(2)}) collective-permute-start(bf16[16,32,128]{2,1,0:T(8,128)(2,1)S(1)} %get-tuple-element.51), channel_id=1, source_target_pairs={{0,4},{2,6},{4,0},{6,2},{8,12},{10,14},{12,8},{14,10},{1,5},{3,7},... | collective-permute-start | bytes 393224 | tf_op jit(solution)/shard_map/ppermute | solution.py:477
  11.9 2.5 %collective-permute-start.4 = (bf16[16,32,128]{2,1,0:T(8,128)(2,1)S(1)}, bf16[16,32,128]{2,1,0:T(8,128)(2,1)S(1)}, u32[]{:S(2)}, u32[]{:S(2)}) collective-permute-start(bf16[16,32,128]{2,1,0:T(8,128)(2,1)S(1)} %get-tuple-element.52), channel_id=1, source_target_pairs={{0,8},{2,10},{4,12},{6,14},{8,0},{10,2},{12,4},{14,6},{1,9},{3,11}... | collective-permute-start | bytes 393224 | tf_op jit(solution)/shard_map/ppermute | solution.py:477
  14.4 1.4 %collective-permute-start.5 = (bf16[16,32,128]{2,1,0:T(8,128)(2,1)S(1)}, bf16[16,32,128]{2,1,0:T(8,128)(2,1)S(1)}, u32[]{:S(2)}, u32[]{:S(2)}) collective-permute-start(bf16[16,32,128]{2,1,0:T(8,128)(2,1)S(1)} %get-tuple-element.53), channel_id=1, source_target_pairs={{0,10},{2,8},{4,14},{6,12},{8,2},{10,0},{12,6},{14,4},{1,11},{3,9}... | collective-permute-start | bytes 393224 | tf_op jit(solution)/shard_map/ppermute | solution.py:477
  15.8 0.3 collective-permute-start.6
  16.1 0.0 collective-permute-done.2.refs_0_
  16.1 3.6 %collective-permute-start.7 = (bf16[16,32,128]{2,1,0:T(8,128)(2,1)S(1)}, bf16[16,32,128]{2,1,0:T(8,128)(2,1)S(1)}, u32[]{:S(2)}, u32[]{:S(2)}) collective-permute-start(bf16[16,32,128]{2,1,0:T(8,128)(2,1)S(1)} %get-tuple-element.55), channel_id=1, source_target_pairs={{0,14},{2,12},{4,10},{6,8},{8,6},{10,4},{12,2},{14,0},{1,15},{3,13... | collective-permute-start | bytes 393224 | tf_op jit(solution)/shard_map/ppermute | solution.py:477
  19.7 0.0 collective-permute-done.3.refs_1_
  19.7 1.6 %collective-permute-start.8 = (bf16[16,32,128]{2,1,0:T(8,128)(2,1)S(1)}, bf16[16,32,128]{2,1,0:T(8,128)(2,1)S(1)}, u32[]{:S(2)}, u32[]{:S(2)}) collective-permute-start(bf16[16,32,128]{2,1,0:T(8,128)(2,1)S(1)} %get-tuple-element.56), channel_id=1, source_target_pairs={{0,12},{2,14},{4,6},{6,4},{8,10},{10,8},{12,0},{14,2},{1,13},{3,15... | collective-permute-start | bytes 393224 | tf_op jit(solution)/shard_map/ppermute | solution.py:477
  21.3 0.3 table.1.refs_8_
  21.6 3.3 %collective-permute-done.4.refs_2_ = bf16[16,32,128]{2,1,0:T(8,128)(2,1)S(1)} collective-permute-done((bf16[16,32,128]{2,1,0:T(8,128)(2,1)S(1)}, bf16[16,32,128]{2,1,0:T(8,128)(2,1)S(1)}, u32[]{:S(2)}, u32[]{:S(2)}) %collective-permute-start.4) | collective-permute-done | bytes 131104 | tf_op jit(solution)/shard_map/ppermute | solution.py:477
  24.9 9.0 %collective-permute-done.5.refs_3_ = bf16[16,32,128]{2,1,0:T(8,128)(2,1)S(1)} collective-permute-done((bf16[16,32,128]{2,1,0:T(8,128)(2,1)S(1)}, bf16[16,32,128]{2,1,0:T(8,128)(2,1)S(1)}, u32[]{:S(2)}, u32[]{:S(2)}) %collective-permute-start.5) | collective-permute-done | bytes 131104 | tf_op jit(solution)/shard_map/ppermute | solution.py:477
  33.9 0.0 collective-permute-done.6.refs_4_
  33.9 0.0 collective-permute-done.7.refs_5_
  33.9 0.0 collective-permute-done.8.refs_6_
  33.9 0.0 copy-done
  33.9 1.4 %peaks.1 = (f32[1,16]{1,0:T(1,128)}, f32[1,16]{1,0:T(1,128)}) custom-call(bf16[16,32,128]{2,1,0:T(8,128)(2,1)S(1)} %collective-permute-done.2.refs_0_, bf16[16,32,128]{2,1,0:T(8,128)(2,1)S(1)} %collective-permute-done.3.refs_1_, bf16[16,32,128]{2,1,0:T(8,128)(2,1)S(1)} %collective-permute-done.4.refs_2_, ...), custom_call_target="tpu_custom_call" | custom-call | tf_op jit(solution)/shard_map/peaks/pallas_call | solution.py:430
Async XLA Ops:
  4.0 2.3 %collective-permute-start.1 = (bf16[16,128,128]{2,1,0:T(8,128)(2,1)S(1)}, bf16[16,128,128]{2,1,0:T(8,128)(2,1)S(1)}, u32[]{:S(2)}, u32[]{:S(2)}) collective-permute-start(bf16[16,128,128]{2,1,0:T(8,128)(2,1)S(1)} %get-tuple-element.49), channel_id=1, source_target_pairs={{0,1},{1,0},{2,3},{3,2},{4,5},{5,4},{6,7},{7,6},{8,9},{9,8},{10,11... | collective-permute-start | bytes 1572872 | tf_op jit(solution)/shard_map/ppermute | solution.py:287
  5.3 2.0 %collective-permute-start = (bf16[16,128,128]{2,1,0:T(8,128)(2,1)S(1)}, bf16[16,128,128]{2,1,0:T(8,128)(2,1)S(1)}, u32[]{:S(2)}, u32[]{:S(2)}) collective-permute-start(bf16[16,128,128]{2,1,0:T(8,128)(2,1)S(1)} %get-tuple-element.48), channel_id=1, source_target_pairs={{0,1},{1,0},{2,3},{3,2},{4,5},{5,4},{6,7},{7,6},{8,9},{9,8},{10,11... | collective-permute-start | bytes 1572872 | tf_op jit(solution)/shard_map/ppermute | solution.py:291
  6.4 27.6 %copy-start = (f32[1,16]{1,0:T(1,128)S(1)}, f32[1,16]{1,0:T(1,128)}, u32[]{:S(2)}) copy-start(f32[1,16]{1,0:T(1,128)} %refs_9_.1) | copy-start | bytes 196
  7.6 8.6 %collective-permute-start.2 = (bf16[16,32,128]{2,1,0:T(8,128)(2,1)S(1)}, bf16[16,32,128]{2,1,0:T(8,128)(2,1)S(1)}, u32[]{:S(2)}, u32[]{:S(2)}) collective-permute-start(bf16[16,32,128]{2,1,0:T(8,128)(2,1)S(1)} %get-tuple-element.50), channel_id=1, source_target_pairs={{0,2},{2,0},{4,8},{6,10},{8,4},{10,6},{12,14},{14,12},{1,3},{3,1},... | collective-permute-start | bytes 393224 | tf_op jit(solution)/shard_map/ppermute | solution.py:477
  10.3 9.4 %collective-permute-start.3 = (bf16[16,32,128]{2,1,0:T(8,128)(2,1)S(1)}, bf16[16,32,128]{2,1,0:T(8,128)(2,1)S(1)}, u32[]{:S(2)}, u32[]{:S(2)}) collective-permute-start(bf16[16,32,128]{2,1,0:T(8,128)(2,1)S(1)} %get-tuple-element.51), channel_id=1, source_target_pairs={{0,4},{2,6},{4,0},{6,2},{8,12},{10,14},{12,8},{14,10},{1,5},{3,7},... | collective-permute-start | bytes 393224 | tf_op jit(solution)/shard_map/ppermute | solution.py:477
  11.9 13.0 %collective-permute-start.4 = (bf16[16,32,128]{2,1,0:T(8,128)(2,1)S(1)}, bf16[16,32,128]{2,1,0:T(8,128)(2,1)S(1)}, u32[]{:S(2)}, u32[]{:S(2)}) collective-permute-start(bf16[16,32,128]{2,1,0:T(8,128)(2,1)S(1)} %get-tuple-element.52), channel_id=1, source_target_pairs={{0,8},{2,10},{4,12},{6,14},{8,0},{10,2},{12,4},{14,6},{1,9},{3,11}... | collective-permute-start | bytes 393224 | tf_op jit(solution)/shard_map/ppermute | solution.py:477
  14.4 19.5 %collective-permute-start.5 = (bf16[16,32,128]{2,1,0:T(8,128)(2,1)S(1)}, bf16[16,32,128]{2,1,0:T(8,128)(2,1)S(1)}, u32[]{:S(2)}, u32[]{:S(2)}) collective-permute-start(bf16[16,32,128]{2,1,0:T(8,128)(2,1)S(1)} %get-tuple-element.53), channel_id=1, source_target_pairs={{0,10},{2,8},{4,14},{6,12},{8,2},{10,0},{12,6},{14,4},{1,11},{3,9}... | collective-permute-start | bytes 393224 | tf_op jit(solution)/shard_map/ppermute | solution.py:477
  15.8 18.1 %collective-permute-start.6 = (bf16[16,32,128]{2,1,0:T(8,128)(2,1)S(1)}, bf16[16,32,128]{2,1,0:T(8,128)(2,1)S(1)}, u32[]{:S(2)}, u32[]{:S(2)}) collective-permute-start(bf16[16,32,128]{2,1,0:T(8,128)(2,1)S(1)} %get-tuple-element.54), channel_id=1, source_target_pairs={{0,6},{2,4},{4,2},{6,0},{8,14},{10,12},{12,10},{14,8},{1,7},{3,5},... | collective-permute-start | bytes 393224 | tf_op jit(solution)/shard_map/ppermute | solution.py:477
  16.1 17.8 %collective-permute-start.7 = (bf16[16,32,128]{2,1,0:T(8,128)(2,1)S(1)}, bf16[16,32,128]{2,1,0:T(8,128)(2,1)S(1)}, u32[]{:S(2)}, u32[]{:S(2)}) collective-permute-start(bf16[16,32,128]{2,1,0:T(8,128)(2,1)S(1)} %get-tuple-element.55), channel_id=1, source_target_pairs={{0,14},{2,12},{4,10},{6,8},{8,6},{10,4},{12,2},{14,0},{1,15},{3,13... | collective-permute-start | bytes 393224 | tf_op jit(solution)/shard_map/ppermute | solution.py:477
  19.7 14.2 %collective-permute-start.8 = (bf16[16,32,128]{2,1,0:T(8,128)(2,1)S(1)}, bf16[16,32,128]{2,1,0:T(8,128)(2,1)S(1)}, u32[]{:S(2)}, u32[]{:S(2)}) collective-permute-start(bf16[16,32,128]{2,1,0:T(8,128)(2,1)S(1)} %get-tuple-element.56), channel_id=1, source_target_pairs={{0,12},{2,14},{4,6},{6,4},{8,10},{10,8},{12,0},{14,2},{1,13},{3,15... | collective-permute-start | bytes 393224 | tf_op jit(solution)/shard_map/ppermute | solution.py:477
where the time goes:
time: 35.5 us; the launch traced here: 35.3 us
  starting transfers between devices  14.4 us (41%)
  waiting for transfers between devices  12.9 us (36%)
  Pallas kernels  7.38 us (21%)
  between operations  0.7 us (2%)
    ppermute x7, starting transfers between devices, body(): lax.ppermute(parts[slot], 'freq', pairs)  13.7 us
    ppermute x7, waiting for transfers between devices, body(): lax.ppermute(parts[slot], 'freq', pairs)  12.3 us
    pallas_call x1, Pallas kernels, partials(): call(functools.partial(other_even_kernel, freq_total, slots), 'other_even...  3.39 us
    pallas_call x1, Pallas kernels, peaks(): pl.pallas_call(functools.partial(peak_kernel, freq_total, folded, sources...  1.37 us
    pallas_call x1, Pallas kernels, partials(): call(own_kernel, 'own', [vmem] * 10, [jax.ShapeDtypeStruct((2 * W_DEV, FG...  0.96 us
  transfers between devices with their start and end apart: 9, of which 3 were waited for; matrix products, arithmetic and copies ran while one was open for 0% of the time, Pallas kernels for 7%

commit v1 on v0

--- a/solution.py
+++ b/solution.py
@@ -49,8 +49,8 @@
 
 def slot_masks(slots):
     half = slots // 2
-    between = (2, half, half + 1, 3, slots - 1)
-    return (0, 1, *between, slots - 2), (0, slots - 2, *between, 1)
+    first, last = (half, half + 1, 2), (3, slots - 1)
+    return (0, *first, 1, *last, slots - 2), (0, *first, slots - 2, *last, 1)
 
 
 def partner(slots, slot):
@@ -233,17 +233,11 @@
     store_spectra(1, picked_ref, law_ref, *k_refs, out_ref, 0)
 
 
-def own_kernel(*refs):
-    picked_refs, refs = refs[:2], refs[2:]
-    even, step, odd, k_refs = (refs[2 * i : 2 * i + 2] for i in range(4))
-    out_ref, law_ref = refs[8:]
-    step = [ref[...] for ref in step]
-    for parity, law in enumerate((even, odd)):
-        store_law(law_ref.at[parity], [ref[...] for ref in law], step)
-    for parity in range(2):
-        store_spectra(
-            parity, picked_refs[parity], law_ref.at[parity], *k_refs, out_ref, parity * W_DEV
-        )
+def own_kernel(parity, picked_ref, *refs):
+    law, step, k_refs = (refs[2 * i : 2 * i + 2] for i in range(3))
+    out_ref, law_ref = refs[-2:]
+    store_law(law_ref, [ref[...] for ref in law], [ref[...] for ref in step])
+    store_spectra(parity, picked_ref, law_ref, *k_refs, out_ref, 0)
 
 
 def call(kernel, name, in_specs, out_shape, scratch):
@@ -289,45 +283,69 @@
         other_odd_kernel, "other_odd", [vmem] * 8, [out, picked], work
     )(field, picks, *kept[:6])
     odd = lax.ppermute(odd, "elem", swap)
-    (own,) = call(
-        own_kernel,
-        "own",
-        [vmem] * 10,
-        [jax.ShapeDtypeStruct((2 * W_DEV, FG, ROWS), jnp.bfloat16)],
-        [pltpu.VMEM((2, *law), jnp.bfloat16)],
-    )(even_picked, odd_picked, *kept[6:])
-    return own, even, odd
-
-
-def total(own_ref, moved_ref, parity, rows):
-    own = own_ref[parity * W_DEV : (parity + 1) * W_DEV, rows]
-    both = own.astype(jnp.float32) + moved_ref[:, rows].astype(jnp.float32)
+    law_even, step, law_odd, factors = (kept[6 + 2 * i : 8 + 2 * i] for i in range(4))
+
+    def own(parity, *after):
+        name, array, base = (
+            ("own_even", even_picked, law_even),
+            ("own_odd", odd_picked, law_odd),
+        )[parity]
+        return call(
+            functools.partial(own_kernel, parity),
+            name,
+            [vmem] * 7 + [pl.BlockSpec(memory_space=pl.ANY)] * len(after),
+            [out],
+            [pltpu.VMEM(law, jnp.bfloat16)],
+        )(array, *base, *step, *factors, *after)[0]
+
+    return own, (even, odd)
+
+
+def total(own_ref, moved_ref, first, size):
+    rows = pl.ds(first, size)
+    both = own_ref[:, rows].astype(jnp.float32) + moved_ref[:, rows].astype(jnp.float32)
     return jnp.swapaxes(both, 0, 1).astype(jnp.bfloat16)
 
 
-def add_even_kernel(size, own_ref, even_ref, held_ref):
-    for first in range(0, held_ref.shape[0], size):
-        rows = pl.ds(first, size)
-        held_ref[rows] = total(own_ref, even_ref, 0, rows)
-
-
-def add_odd_kernel(own_ref, odd_ref, held_ref, *refs):
-    size = refs[0].shape[0]
-    for slot, ref in enumerate(refs):
-        rows = pl.ds(slot * size, size)
-        ref[:, :W_DEV] = held_ref[rows]
-        ref[:, W_DEV:] = total(own_ref, odd_ref, 1, rows)
-
-
-def add(own, even, odd, slots):
+def add_even_kernel(size, early, own_ref, moved_ref, held_ref, *refs):
+    slots = range(own_ref.shape[1] // size)
+    for slot, ref in zip(early, refs):
+        ref[...] = total(own_ref, moved_ref, slot * size, size)
+    for i, slot in enumerate([s for s in slots if s not in early]):
+        held_ref[pl.ds(i * size, size)] = total(own_ref, moved_ref, slot * size, size)
+
+
+def add_even(own, moved, size, early):
     vmem = pl.BlockSpec(memory_space=pltpu.VMEM)
     planes, flaws, rows = own.shape
-    size = flaws // slots
-    shape = jax.ShapeDtypeStruct((flaws, planes // 2, rows), own.dtype)
-    kernel = functools.partial(add_even_kernel, min(size, 16))
-    (held,) = call(kernel, "add_even", [vmem] * 2, [shape], [])(own, even)
-    shapes = [jax.ShapeDtypeStruct((size, planes, rows), own.dtype)] * slots
-    return call(add_odd_kernel, "add_odd", [vmem] * 3, shapes, [])(own, odd, held)
+    shapes = [jax.ShapeDtypeStruct((flaws - size * len(early), planes, rows), own.dtype)]
+    shapes += [jax.ShapeDtypeStruct((size, planes, rows), own.dtype)] * len(early)
+    return call(
+        functools.partial(add_even_kernel, size, early), "add_even", [vmem] * 2, shapes, []
+    )(own, moved)
+
+
+def add_odd_kernel(size, early, late, own_ref, moved_ref, held_ref, *refs):
+    held = sorted(late)
+    for slot, ref in zip((*early, *late), refs):
+        value = total(own_ref, moved_ref, slot * size, size)
+        if slot in early:
+            ref[...] = value
+        else:
+            ref[:, :W_DEV] = held_ref[pl.ds(held.index(slot) * size, size)]
+            ref[:, W_DEV:] = value
+
+
+def add_odd(own, moved, held, size, early, late):
+    vmem = pl.BlockSpec(memory_space=pltpu.VMEM)
+    planes, _, rows = own.shape
+    shapes = [
+        jax.ShapeDtypeStruct((size, planes * (1 if slot in early else 2), rows), own.dtype)
+        for slot in (*early, *late)
+    ]
+    return call(
+        functools.partial(add_odd_kernel, size, early, late), "add_odd", [vmem] * 3, shapes, []
+    )(own, moved, held)
 
 
 def table_kernel(freq_total, slots, table_ref):
@@ -381,13 +399,12 @@
     for first in range(0, columns, width):
         parts = []
         for parity in range(2):
-            planes = slice(parity * W_DEV, (parity + 1) * W_DEV)
             spectra = jnp.concatenate(
                 [
                     jnp.concatenate(
                         [
-                            refs[i][row + first + k, planes, :]
-                            for i, row in sources
+                            refs[i][row + first + k, plane : plane + W_DEV, :]
+                            for i, row, plane in sources[parity]
                         ]
                         * 2,
                         axis=0,
@@ -468,20 +485,41 @@
     times = sample_count // 2 if folded else sample_count
     twiddles = table(freq_total, slots, times, min(128, times))
     field = beam_field.reshape(W_HALF, 2, *beam_field.shape[1:])
-    parts = add(*partials(field, small, swap, freq_total, slots), slots)
+    own, moved = partials(field, small, swap, freq_total, slots)
+    size = FG // slots
+    early = (1, 2) if direct else ()
+    late = tuple(slot for slot in range(slots) if slot not in early)
+    held, *even = add_even(own(0), moved[0], size, early)
+    odd = add_odd(own(1, held), moved[1], held, size, early, late)
     if direct:
         half = slots // 2
-        spectra = []
-        for slot, masks in enumerate(zip(*slot_masks(slots))):
+
+        def send(array, slot):
+            masks = [masks[slot] for masks in slot_masks(slots)]
             pairs = [(a, a ^ masks[((2 * a) ^ a) & half != 0]) for a in range(slots)]
-            spectra.append(lax.ppermute(parts[slot], "freq", pairs) if slot else parts[slot])
-        spectra = [*spectra[1:], spectra[0]]
-        sources = [((slot - 1) % slots, 0) for slot in range(slots)]
+            return lax.ppermute(array, "freq", pairs) if slot else array
+
+        even = {slot: send(array, slot) for slot, array in zip(early, even)}
+        rest = {slot: send(array, slot) for slot, array in zip((*early, *late), odd)}
+        order = (4, 3, 6, 5, 7, 1, 2, 0)
+        spectra = [*even.values(), *(rest[slot] for slot in order)]
+        sources = [
+            [
+                (early.index(slot), 0, 0)
+                if slot in early and parity == 0
+                else (len(early) + order.index(slot), 0, 0 if slot in early else plane)
+                for slot in range(slots)
+            ]
+            for parity, plane in enumerate((0, W_DEV))
+        ]
     else:
         spectra = [
-            lax.all_to_all(parts[0], "freq", split_axis=0, concat_axis=0, tiled=True)
+            lax.all_to_all(odd[0], "freq", split_axis=0, concat_axis=0, tiled=True)
         ]
-        sources = [(0, s * (FG // freq_count)) for s in range(freq_count)]
+        columns = FG // freq_count
+        sources = [
+            [(0, s * columns, plane) for s in range(freq_count)] for plane in (0, W_DEV)
+        ]
     return tuple(peaks(spectra, sources, twiddles, noise_level, freq_total, folded))
 
 

time: 35.5 us -> 36 us (1.014)
  the two profiles are of different devices: /device:TPU:0 before, /device:TPU:12 now
where the time goes in v1:
time: 36 us; the launch traced here: 35.8 us
  starting transfers between devices  16.7 us (46%)
  waiting for transfers between devices  11 us (31%)
  Pallas kernels  7.37 us (20%)
  between operations  0.7 us (2%)
    ppermute x9, starting transfers between devices, send(): return lax.ppermute(array, 'freq', pairs) if slot else array  16.1 us
    ppermute x9, waiting for transfers between devices, send(): return lax.ppermute(array, 'freq', pairs) if slot else array  10.9 us
    pallas_call x1, Pallas kernels, partials(): call(functools.partial(other_even_kernel, freq_total, slots), 'other_even...  3.38 us
    pallas_call x1, Pallas kernels, peaks(): pl.pallas_call(functools.partial(peak_kernel, freq_total, folded, sources...  1.37 us
    pallas_call x2, Pallas kernels, own(): call(functools.partial(own_kernel, parity), name, [vmem] * 7 + [pl.BlockS...  0.96 us
  transfers between devices with their start and end apart: 11, of which 6 were waited for; matrix products, arithmetic and copies ran while one was open for 0% of the time, Pallas kernels for 7%

profile of v1, /device:TPU:12, one launch (start us, length us, event | category | flops | bytes accessed | tf_op | source)
XLA Modules:
  0.0 35.8 jit_solution(11842300767511165733)
XLA Ops:
  0.6 3.4 %other_even.1 = (bf16[16,128,128]{2,1,0:T(8,128)(2,1)S(1)}, bf16[8,128,256]{2,1,0:T(8,128)(2,1)S(1)}, bf16[8,2,2,128,256]{4,3,2,1,0:T(8,128)(2,1)S(1)}, bf16[256...) custom-call(bf16[8,2,2,128,256]{4,3,2,1,0:T(8,128)(2,1)} %bitcast.3,, ...), custom_call_target="tpu_custom_call" | custom-call | flops 1000 | bytes 1000 | tf_op jit(solution)/shard_map/other_even/pallas_call | solution.py:270
  4.0 0.1 collective-permute-start
  4.1 0.7 %other_odd.1 = (bf16[16,128,128]{2,1,0:T(8,128)(2,1)S(1)}, bf16[8,128,256]{2,1,0:T(8,128)(2,1)S(1)}) custom-call(bf16[8,2,2,128,256]{4,3,2,1,0:T(8,128)(2,1)S(1)} %get-tuple-element.43.field_ref, bf16[256,256]{1,0:T(8,128)(2,1)S(1)} %get-tuple-element.44.picks_ref, f32[128,128]{1,0:T(8,128)S(1)} %get-tuple-element.45.refs_0_, ...), custom_call_target="tpu_custom_call" | custom-call | flops 1000 | bytes 1000 | tf_op jit(solution)/shard_map/other_odd/pallas_call | solution.py:282
  4.8 0.6 %collective-permute-start.3 = (bf16[16,128,128]{2,1,0:T(8,128)(2,1)S(1)}, bf16[16,128,128]{2,1,0:T(8,128)(2,1)S(1)}, u32[]{:S(2)}, u32[]{:S(2)}) collective-permute-start(bf16[16,128,128]{2,1,0:T(8,128)(2,1)S(1)} %get-tuple-element.55), channel_id=1, source_target_pairs={{0,1},{1,0},{2,3},{3,2},{4,5},{5,4},{6,7},{7,6},{8,9},{9,8},{10,11... | collective-permute-start | bytes 1572872 | tf_op jit(solution)/shard_map/ppermute | solution.py:285
  5.4 0.5 %own_even.1.own_ref = bf16[16,128,128]{2,1,0:T(8,128)(2,1)S(1)} custom-call(bf16[8,128,256]{2,1,0:T(8,128)(2,1)S(1)} %get-tuple-element.33.picked_ref, f32[128,128]{1,0:T(8,128)S(1)} %get-tuple-element.34.refs_0_, f32[128,128]{1,0:T(8,128)S(1)} %get-tuple-element.35.refs_1_, f32[128,128]{1,0:T(8,128)S(1)} %get-tuple-element.36.refs_2_, ...), custom_call_target="tpu_custom_call" | custom-call | flops 1000 | bytes 1000 | tf_op jit(solution)/shard_map/own_even/pallas_call | solution.py:293
  5.9 0.0 copy-start
  5.9 0.1 collective-permute-done.moved_ref
  6.0 0.3 add_even.1
  6.3 2.7 %collective-permute-start.1 = (bf16[16,16,128]{2,1,0:T(8,128)(2,1)S(1)}, bf16[16,16,128]{2,1,0:T(8,128)(2,1)S(1)}, u32[]{:S(2)}, u32[]{:S(2)}) collective-permute-start(bf16[16,16,128]{2,1,0:T(8,128)(2,1)S(1)} %get-tuple-element.41), channel_id=1, source_target_pairs={{0,8},{2,10},{4,12},{6,14},{8,0},{10,2},{12,4},{14,6},{1,9},{3,11}... | collective-permute-start | bytes 196616 | tf_op jit(solution)/shard_map/ppermute | solution.py:500
  9.0 1.3 %collective-permute-start.2 = (bf16[16,16,128]{2,1,0:T(8,128)(2,1)S(1)}, bf16[16,16,128]{2,1,0:T(8,128)(2,1)S(1)}, u32[]{:S(2)}, u32[]{:S(2)}) collective-permute-start(bf16[16,16,128]{2,1,0:T(8,128)(2,1)S(1)} %get-tuple-element.42), channel_id=1, source_target_pairs={{0,10},{2,8},{4,14},{6,12},{8,2},{10,0},{12,6},{14,4},{1,11},{3,9}... | collective-permute-start | bytes 196616 | tf_op jit(solution)/shard_map/ppermute | solution.py:500
  10.2 0.5 %own_odd.1.own_ref = bf16[16,128,128]{2,1,0:T(8,128)(2,1)S(1)} custom-call(bf16[8,128,256]{2,1,0:T(8,128)(2,1)S(1)} %get-tuple-element.51.picked_ref, f32[128,128]{1,0:T(8,128)S(1)} %get-tuple-element.52.refs_0_, f32[128,128]{1,0:T(8,128)S(1)} %get-tuple-element.53.refs_1_, f32[128,128]{1,0:T(8,128)S(1)} %get-tuple-element.36.refs_2_, ...), custom_call_target="tpu_custom_call" | custom-call | flops 1000 | bytes 1000 | tf_op jit(solution)/shard_map/own_odd/pallas_call | solution.py:293
  10.7 0.0 collective-permute-done.3.moved_ref
  10.7 0.3 add_odd.1
  11.0 2.7 %collective-permute-start.9 = (bf16[16,16,128]{2,1,0:T(8,128)(2,1)S(1)}, bf16[16,16,128]{2,1,0:T(8,128)(2,1)S(1)}, u32[]{:S(2)}, u32[]{:S(2)}) collective-permute-start(bf16[16,16,128]{2,1,0:T(8,128)(2,1)S(1)} %get-tuple-element.61), channel_id=1, source_target_pairs={{0,8},{2,10},{4,12},{6,14},{8,0},{10,2},{12,4},{14,6},{1,9},{3,11}... | collective-permute-start | bytes 196616 | tf_op jit(solution)/shard_map/ppermute | solution.py:500
  13.7 0.3 collective-permute-start.10
  14.0 1.6 %collective-permute-start.4 = (bf16[16,32,128]{2,1,0:T(8,128)(2,1)S(1)}, bf16[16,32,128]{2,1,0:T(8,128)(2,1)S(1)}, u32[]{:S(2)}, u32[]{:S(2)}) collective-permute-start(bf16[16,32,128]{2,1,0:T(8,128)(2,1)S(1)} %get-tuple-element.56), channel_id=1, source_target_pairs={{0,2},{2,0},{4,8},{6,10},{8,4},{10,6},{12,14},{14,12},{1,3},{3,1},... | collective-permute-start | bytes 393224 | tf_op jit(solution)/shard_map/ppermute | solution.py:500
  15.6 0.0 collective-permute-done.1.refs_0_
  15.6 0.4 %collective-permute-start.5 = (bf16[16,32,128]{2,1,0:T(8,128)(2,1)S(1)}, bf16[16,32,128]{2,1,0:T(8,128)(2,1)S(1)}, u32[]{:S(2)}, u32[]{:S(2)}) collective-permute-start(bf16[16,32,128]{2,1,0:T(8,128)(2,1)S(1)} %get-tuple-element.57), channel_id=1, source_target_pairs={{0,4},{2,6},{4,0},{6,2},{8,12},{10,14},{12,8},{14,10},{1,5},{3,7},... | collective-permute-start | bytes 393224 | tf_op jit(solution)/shard_map/ppermute | solution.py:500
  16.0 1.7 %collective-permute-done.2.refs_1_ = bf16[16,16,128]{2,1,0:T(8,128)(2,1)S(1)} collective-permute-done((bf16[16,16,128]{2,1,0:T(8,128)(2,1)S(1)}, bf16[16,16,128]{2,1,0:T(8,128)(2,1)S(1)}, u32[]{:S(2)}, u32[]{:S(2)}) %collective-permute-start.2) | collective-permute-done | bytes 65568 | tf_op jit(solution)/shard_map/ppermute | solution.py:500
  17.7 3.4 %collective-permute-start.6 = (bf16[16,32,128]{2,1,0:T(8,128)(2,1)S(1)}, bf16[16,32,128]{2,1,0:T(8,128)(2,1)S(1)}, u32[]{:S(2)}, u32[]{:S(2)}) collective-permute-start(bf16[16,32,128]{2,1,0:T(8,128)(2,1)S(1)} %get-tuple-element.58), channel_id=1, source_target_pairs={{0,14},{2,12},{4,10},{6,8},{8,6},{10,4},{12,2},{14,0},{1,15},{3,13... | collective-permute-start | bytes 393224 | tf_op jit(solution)/shard_map/ppermute | solution.py:500
  21.1 0.0 collective-permute-done.9.refs_7_
  21.1 3.2 %collective-permute-start.7 = (bf16[16,32,128]{2,1,0:T(8,128)(2,1)S(1)}, bf16[16,32,128]{2,1,0:T(8,128)(2,1)S(1)}, u32[]{:S(2)}, u32[]{:S(2)}) collective-permute-start(bf16[16,32,128]{2,1,0:T(8,128)(2,1)S(1)} %get-tuple-element.59), channel_id=1, source_target_pairs={{0,6},{2,4},{4,2},{6,0},{8,14},{10,12},{12,10},{14,8},{1,7},{3,5},... | collective-permute-start | bytes 393224 | tf_op jit(solution)/shard_map/ppermute | solution.py:500
  24.3 0.0 collective-permute-done.10.refs_8_
  24.3 0.6 %collective-permute-start.8 = (bf16[16,32,128]{2,1,0:T(8,128)(2,1)S(1)}, bf16[16,32,128]{2,1,0:T(8,128)(2,1)S(1)}, u32[]{:S(2)}, u32[]{:S(2)}) collective-permute-start(bf16[16,32,128]{2,1,0:T(8,128)(2,1)S(1)} %get-tuple-element.60), channel_id=1, source_target_pairs={{0,12},{2,14},{4,6},{6,4},{8,10},{10,8},{12,0},{14,2},{1,13},{3,15... | collective-permute-start | bytes 393224 | tf_op jit(solution)/shard_map/ppermute | solution.py:500
  25.0 0.3 table.1.refs_10_
  25.3 3.1 %collective-permute-done.4.refs_2_ = bf16[16,32,128]{2,1,0:T(8,128)(2,1)S(1)} collective-permute-done((bf16[16,32,128]{2,1,0:T(8,128)(2,1)S(1)}, bf16[16,32,128]{2,1,0:T(8,128)(2,1)S(1)}, u32[]{:S(2)}, u32[]{:S(2)}) %collective-permute-start.4) | collective-permute-done | bytes 131104 | tf_op jit(solution)/shard_map/ppermute | solution.py:500
  28.3 0.0 collective-permute-done.5.refs_3_
  28.3 3.3 %collective-permute-done.6.refs_4_ = bf16[16,32,128]{2,1,0:T(8,128)(2,1)S(1)} collective-permute-done((bf16[16,32,128]{2,1,0:T(8,128)(2,1)S(1)}, bf16[16,32,128]{2,1,0:T(8,128)(2,1)S(1)}, u32[]{:S(2)}, u32[]{:S(2)}) %collective-permute-start.6) | collective-permute-done | bytes 131104 | tf_op jit(solution)/shard_map/ppermute | solution.py:500
  31.6 0.4 %collective-permute-done.7.refs_5_ = bf16[16,32,128]{2,1,0:T(8,128)(2,1)S(1)} collective-permute-done((bf16[16,32,128]{2,1,0:T(8,128)(2,1)S(1)}, bf16[16,32,128]{2,1,0:T(8,128)(2,1)S(1)}, u32[]{:S(2)}, u32[]{:S(2)}) %collective-permute-start.7) | collective-permute-done | bytes 131104 | tf_op jit(solution)/shard_map/ppermute | solution.py:500
  32.1 2.3 %collective-permute-done.8.refs_6_ = bf16[16,32,128]{2,1,0:T(8,128)(2,1)S(1)} collective-permute-done((bf16[16,32,128]{2,1,0:T(8,128)(2,1)S(1)}, bf16[16,32,128]{2,1,0:T(8,128)(2,1)S(1)}, u32[]{:S(2)}, u32[]{:S(2)}) %collective-permute-start.8) | collective-permute-done | bytes 131104 | tf_op jit(solution)/shard_map/ppermute | solution.py:500
  34.4 0.0 copy-done
  34.4 1.4 %peaks.1 = (f32[1,16]{1,0:T(1,128)}, f32[1,16]{1,0:T(1,128)}) custom-call(bf16[16,16,128]{2,1,0:T(8,128)(2,1)S(1)} %collective-permute-done.1.refs_0_, bf16[16,16,128]{2,1,0:T(8,128)(2,1)S(1)} %collective-permute-done.2.refs_1_, bf16[16,32,128]{2,1,0:T(8,128)(2,1)S(1)} %collective-permute-done.4.refs_2_, ...), custom_call_target="tpu_custom_call" | custom-call | tf_op jit(solution)/shard_map/peaks/pallas_call | solution.py:447
Async XLA Ops:
  4.0 2.0 %collective-permute-start = (bf16[16,128,128]{2,1,0:T(8,128)(2,1)S(1)}, bf16[16,128,128]{2,1,0:T(8,128)(2,1)S(1)}, u32[]{:S(2)}, u32[]{:S(2)}) collective-permute-start(bf16[16,128,128]{2,1,0:T(8,128)(2,1)S(1)} %get-tuple-element.40), channel_id=1, source_target_pairs={{0,1},{1,0},{2,3},{3,2},{4,5},{5,4},{6,7},{7,6},{8,9},{9,8},{10,11... | collective-permute-start | bytes 1572872 | tf_op jit(solution)/shard_map/ppermute | solution.py:281
  4.8 5.9 %collective-permute-start.3 = (bf16[16,128,128]{2,1,0:T(8,128)(2,1)S(1)}, bf16[16,128,128]{2,1,0:T(8,128)(2,1)S(1)}, u32[]{:S(2)}, u32[]{:S(2)}) collective-permute-start(bf16[16,128,128]{2,1,0:T(8,128)(2,1)S(1)} %get-tuple-element.55), channel_id=1, source_target_pairs={{0,1},{1,0},{2,3},{3,2},{4,5},{5,4},{6,7},{7,6},{8,9},{9,8},{10,11... | collective-permute-start | bytes 1572872 | tf_op jit(solution)/shard_map/ppermute | solution.py:285
  5.9 28.6 %copy-start = (f32[1,16]{1,0:T(1,128)S(1)}, f32[1,16]{1,0:T(1,128)}, u32[]{:S(2)}) copy-start(f32[1,16]{1,0:T(1,128)} %refs_11_.1) | copy-start | bytes 196
  6.3 9.3 %collective-permute-start.1 = (bf16[16,16,128]{2,1,0:T(8,128)(2,1)S(1)}, bf16[16,16,128]{2,1,0:T(8,128)(2,1)S(1)}, u32[]{:S(2)}, u32[]{:S(2)}) collective-permute-start(bf16[16,16,128]{2,1,0:T(8,128)(2,1)S(1)} %get-tuple-element.41), channel_id=1, source_target_pairs={{0,8},{2,10},{4,12},{6,14},{8,0},{10,2},{12,4},{14,6},{1,9},{3,11}... | collective-permute-start | bytes 196616 | tf_op jit(solution)/shard_map/ppermute | solution.py:500
  9.0 8.7 %collective-permute-start.2 = (bf16[16,16,128]{2,1,0:T(8,128)(2,1)S(1)}, bf16[16,16,128]{2,1,0:T(8,128)(2,1)S(1)}, u32[]{:S(2)}, u32[]{:S(2)}) collective-permute-start(bf16[16,16,128]{2,1,0:T(8,128)(2,1)S(1)} %get-tuple-element.42), channel_id=1, source_target_pairs={{0,10},{2,8},{4,14},{6,12},{8,2},{10,0},{12,6},{14,4},{1,11},{3,9}... | collective-permute-start | bytes 196616 | tf_op jit(solution)/shard_map/ppermute | solution.py:500
  11.0 10.0 %collective-permute-start.9 = (bf16[16,16,128]{2,1,0:T(8,128)(2,1)S(1)}, bf16[16,16,128]{2,1,0:T(8,128)(2,1)S(1)}, u32[]{:S(2)}, u32[]{:S(2)}) collective-permute-start(bf16[16,16,128]{2,1,0:T(8,128)(2,1)S(1)} %get-tuple-element.61), channel_id=1, source_target_pairs={{0,8},{2,10},{4,12},{6,14},{8,0},{10,2},{12,4},{14,6},{1,9},{3,11}... | collective-permute-start | bytes 196616 | tf_op jit(solution)/shard_map/ppermute | solution.py:500
  13.7 10.6 %collective-permute-start.10 = (bf16[16,16,128]{2,1,0:T(8,128)(2,1)S(1)}, bf16[16,16,128]{2,1,0:T(8,128)(2,1)S(1)}, u32[]{:S(2)}, u32[]{:S(2)}) collective-permute-start(bf16[16,16,128]{2,1,0:T(8,128)(2,1)S(1)} %get-tuple-element.62), channel_id=1, source_target_pairs={{0,10},{2,8},{4,14},{6,12},{8,2},{10,0},{12,6},{14,4},{1,11},{3,9}... | collective-permute-start | bytes 196616 | tf_op jit(solution)/shard_map/ppermute | solution.py:500
  14.0 14.3 %collective-permute-start.4 = (bf16[16,32,128]{2,1,0:T(8,128)(2,1)S(1)}, bf16[16,32,128]{2,1,0:T(8,128)(2,1)S(1)}, u32[]{:S(2)}, u32[]{:S(2)}) collective-permute-start(bf16[16,32,128]{2,1,0:T(8,128)(2,1)S(1)} %get-tuple-element.56), channel_id=1, source_target_pairs={{0,2},{2,0},{4,8},{6,10},{8,4},{10,6},{12,14},{14,12},{1,3},{3,1},... | collective-permute-start | bytes 393224 | tf_op jit(solution)/shard_map/ppermute | solution.py:500
  15.6 12.8 %collective-permute-start.5 = (bf16[16,32,128]{2,1,0:T(8,128)(2,1)S(1)}, bf16[16,32,128]{2,1,0:T(8,128)(2,1)S(1)}, u32[]{:S(2)}, u32[]{:S(2)}) collective-permute-start(bf16[16,32,128]{2,1,0:T(8,128)(2,1)S(1)} %get-tuple-element.57), channel_id=1, source_target_pairs={{0,4},{2,6},{4,0},{6,2},{8,12},{10,14},{12,8},{14,10},{1,5},{3,7},... | collective-permute-start | bytes 393224 | tf_op jit(solution)/shard_map/ppermute | solution.py:500
  17.7 14.0 %collective-permute-start.6 = (bf16[16,32,128]{2,1,0:T(8,128)(2,1)S(1)}, bf16[16,32,128]{2,1,0:T(8,128)(2,1)S(1)}, u32[]{:S(2)}, u32[]{:S(2)}) collective-permute-start(bf16[16,32,128]{2,1,0:T(8,128)(2,1)S(1)} %get-tuple-element.58), channel_id=1, source_target_pairs={{0,14},{2,12},{4,10},{6,8},{8,6},{10,4},{12,2},{14,0},{1,15},{3,13... | collective-permute-start | bytes 393224 | tf_op jit(solution)/shard_map/ppermute | solution.py:500
  21.1 11.0 %collective-permute-start.7 = (bf16[16,32,128]{2,1,0:T(8,128)(2,1)S(1)}, bf16[16,32,128]{2,1,0:T(8,128)(2,1)S(1)}, u32[]{:S(2)}, u32[]{:S(2)}) collective-permute-start(bf16[16,32,128]{2,1,0:T(8,128)(2,1)S(1)} %get-tuple-element.59), channel_id=1, source_target_pairs={{0,6},{2,4},{4,2},{6,0},{8,14},{10,12},{12,10},{14,8},{1,7},{3,5},... | collective-permute-start | bytes 393224 | tf_op jit(solution)/shard_map/ppermute | solution.py:500
  24.3 10.1 %collective-permute-start.8 = (bf16[16,32,128]{2,1,0:T(8,128)(2,1)S(1)}, bf16[16,32,128]{2,1,0:T(8,128)(2,1)S(1)}, u32[]{:S(2)}, u32[]{:S(2)}) collective-permute-start(bf16[16,32,128]{2,1,0:T(8,128)(2,1)S(1)} %get-tuple-element.60), channel_id=1, source_target_pairs={{0,12},{2,14},{4,6},{6,4},{8,10},{10,8},{12,0},{14,2},{1,13},{3,15... | collective-permute-start | bytes 393224 | tf_op jit(solution)/shard_map/ppermute | solution.py:500

commit v2 on v0

--- a/solution.py
+++ b/solution.py
@@ -366,14 +366,19 @@
     )()
 
 
-def peak_kernel(freq_total, folded, sources, *refs):
+def peak_kernel(freq_total, folded, sources, blocks, *refs):
+    def first_step():
+        return blocks == 1 or pl.program_id(0) == 0
+
+    def last_step():
+        return blocks == 1 or pl.program_id(0) == blocks - 1
+
     count = len(refs) - 5
     table_ref, noise_ref, peak_ref, found_ref, best_ref = refs[count:]
-    step = pl.program_id(0)
     columns = peak_ref.shape[1]
     time_block = table_ref.shape[2] // 2
 
-    @pl.when(step == 0)
+    @pl.when(first_step())
     def _():
         best_ref[...] = jnp.zeros_like(best_ref)
 
@@ -410,7 +415,7 @@
                 best_ref[row, :], power[:, k * ROWS : (k + 1) * ROWS]
             )
 
-    @pl.when(step == pl.num_programs(0) - 1)
+    @pl.when(last_step())
     def _():
         largest = jnp.max(best_ref[...], axis=1, keepdims=True)
         shape = best_ref.shape
@@ -426,12 +431,22 @@
 
 def peaks(spectra, sources, twiddles, noise_level, freq_total, folded):
     columns = noise_level.shape[1]
-    out_spec = pl.BlockSpec((1, columns), lambda i: (0, 0))
+    blocks = twiddles.shape[0]
+    if blocks == 1:
+        vmem = pl.BlockSpec(memory_space=pltpu.VMEM)
+        grid, in_specs, out_spec = (), [vmem] * (len(spectra) + 2), vmem
+    else:
+        grid = (blocks,)
+        out_spec = pl.BlockSpec((1, columns), lambda i: (0, 0))
+        in_specs = [pl.BlockSpec(a.shape, lambda i: (0, 0, 0)) for a in spectra]
+        in_specs += [
+            pl.BlockSpec((1, *twiddles.shape[1:]), lambda i: (i, 0, 0, 0)),
+            out_spec,
+        ]
     return pl.pallas_call(
-        functools.partial(peak_kernel, freq_total, folded, sources),
-        grid=(twiddles.shape[0],),
-        in_specs=[pl.BlockSpec(a.shape, lambda i: (0, 0, 0)) for a in spectra]
-        + [pl.BlockSpec((1, *twiddles.shape[1:]), lambda i: (i, 0, 0, 0)), out_spec],
+        functools.partial(peak_kernel, freq_total, folded, sources, blocks),
+        grid=grid,
+        in_specs=in_specs,
         out_specs=[out_spec, out_spec],
         out_shape=[jax.ShapeDtypeStruct((1, columns), jnp.float32)] * 2,
         scratch_shapes=[pltpu.VMEM((max(8, columns), ROWS), jnp.float32)],

time: 35.5 us -> 35.5 us (level)
  no operation moved by 1% of the time
where the time goes in v2:
time: 35.5 us; the launch traced here: 35.3 us
  starting transfers between devices  14.4 us (41%)
  waiting for transfers between devices  12.9 us (36%)
  Pallas kernels  7.38 us (21%)
  between operations  0.7 us (2%)
    ppermute x7, starting transfers between devices, body(): lax.ppermute(parts[slot], 'freq', pairs)  13.7 us
    ppermute x7, waiting for transfers between devices, body(): lax.ppermute(parts[slot], 'freq', pairs)  12.3 us
    pallas_call x1, Pallas kernels, partials(): call(functools.partial(other_even_kernel, freq_total, slots), 'other_even...  3.39 us
    pallas_call x1, Pallas kernels, peaks(): pl.pallas_call(functools.partial(peak_kernel, freq_total, folded, sources...  1.37 us
    pallas_call x1, Pallas kernels, partials(): call(own_kernel, 'own', [vmem] * 10, [jax.ShapeDtypeStruct((2 * W_DEV, FG...  0.96 us
  transfers between devices with their start and end apart: 9, of which 3 were waited for; matrix products, arithmetic and copies ran while one was open for 0% of the time, Pallas kernels for 7%

profile of v2, /device:TPU:0, one launch (start us, length us, event | category | flops | bytes accessed | tf_op | source)
XLA Modules:
  0.0 35.3 jit_solution(6457872437138371167)
XLA Ops:
  0.6 3.4 %other_even.1 = (bf16[16,128,128]{2,1,0:T(8,128)(2,1)S(1)}, bf16[8,128,256]{2,1,0:T(8,128)(2,1)S(1)}, bf16[8,2,2,128,256]{4,3,2,1,0:T(8,128)(2,1)S(1)}, bf16[256...) custom-call(bf16[8,2,2,128,256]{4,3,2,1,0:T(8,128)(2,1)} %bitcast.3,, ...), custom_call_target="tpu_custom_call" | custom-call | flops 1000 | bytes 1000 | tf_op jit(solution)/shard_map/other_even/pallas_call | solution.py:276
  4.0 0.5 %collective-permute-start.1 = (bf16[16,128,128]{2,1,0:T(8,128)(2,1)S(1)}, bf16[16,128,128]{2,1,0:T(8,128)(2,1)S(1)}, u32[]{:S(2)}, u32[]{:S(2)}) collective-permute-start(bf16[16,128,128]{2,1,0:T(8,128)(2,1)S(1)} %get-tuple-element.49), channel_id=1, source_target_pairs={{0,1},{1,0},{2,3},{3,2},{4,5},{5,4},{6,7},{7,6},{8,9},{9,8},{10,11... | collective-permute-start | bytes 1572872 | tf_op jit(solution)/shard_map/ppermute | solution.py:287
  4.5 0.7 %other_odd.1 = (bf16[16,128,128]{2,1,0:T(8,128)(2,1)S(1)}, bf16[8,128,256]{2,1,0:T(8,128)(2,1)S(1)}) custom-call(bf16[8,2,2,128,256]{4,3,2,1,0:T(8,128)(2,1)S(1)} %get-tuple-element.31.field_ref, bf16[256,256]{1,0:T(8,128)(2,1)S(1)} %get-tuple-element.32.picks_ref, f32[128,128]{1,0:T(8,128)S(1)} %get-tuple-element.33.refs_0_, ...), custom_call_target="tpu_custom_call" | custom-call | flops 1000 | bytes 1000 | tf_op jit(solution)/shard_map/other_odd/pallas_call | solution.py:288
  5.3 0.1 collective-permute-start
  5.4 1.0 %own.1.own_ref = bf16[32,128,128]{2,1,0:T(8,128)(2,1)S(1)} custom-call(bf16[8,128,256]{2,1,0:T(8,128)(2,1)S(1)} %get-tuple-element.30.refs_0_, bf16[8,128,256]{2,1,0:T(8,128)(2,1)S(1)} %get-tuple-element.39.refs_1_, f32[128,128]{1,0:T(8,128)S(1)} %get-tuple-element.40.refs_2_, f32[128,128]{1,0:T(8,128)S(1)} %get-tuple-element.41.refs_3_, ...), custom_call_target="tpu_custom_call" | custom-call | flops 1000 | bytes 1000 | tf_op jit(solution)/shard_map/own/pallas_call | solution.py:292
  6.4 0.0 copy-start
  6.4 0.0 collective-permute-done.1.even_ref
  6.4 0.3 add_even.1.held_ref
  6.7 0.5 %collective-permute-done.odd_ref = bf16[16,128,128]{2,1,0:T(8,128)(2,1)S(1)} collective-permute-done((bf16[16,128,128]{2,1,0:T(8,128)(2,1)S(1)}, bf16[16,128,128]{2,1,0:T(8,128)(2,1)S(1)}, u32[]{:S(2)}, u32[]{:S(2)}) %collective-permute-start) | collective-permute-done | bytes 524320 | tf_op jit(solution)/shard_map/ppermute | solution.py:291
  7.2 0.3 add_odd.1
  7.6 2.7 %collective-permute-start.2 = (bf16[16,32,128]{2,1,0:T(8,128)(2,1)S(1)}, bf16[16,32,128]{2,1,0:T(8,128)(2,1)S(1)}, u32[]{:S(2)}, u32[]{:S(2)}) collective-permute-start(bf16[16,32,128]{2,1,0:T(8,128)(2,1)S(1)} %get-tuple-element.50), channel_id=1, source_target_pairs={{0,2},{2,0},{4,8},{6,10},{8,4},{10,6},{12,14},{14,12},{1,3},{3,1},... | collective-permute-start | bytes 393224 | tf_op jit(solution)/shard_map/ppermute | solution.py:492
  10.3 1.7 %collective-permute-start.3 = (bf16[16,32,128]{2,1,0:T(8,128)(2,1)S(1)}, bf16[16,32,128]{2,1,0:T(8,128)(2,1)S(1)}, u32[]{:S(2)}, u32[]{:S(2)}) collective-permute-start(bf16[16,32,128]{2,1,0:T(8,128)(2,1)S(1)} %get-tuple-element.51), channel_id=1, source_target_pairs={{0,4},{2,6},{4,0},{6,2},{8,12},{10,14},{12,8},{14,10},{1,5},{3,7},... | collective-permute-start | bytes 393224 | tf_op jit(solution)/shard_map/ppermute | solution.py:492
  11.9 2.5 %collective-permute-start.4 = (bf16[16,32,128]{2,1,0:T(8,128)(2,1)S(1)}, bf16[16,32,128]{2,1,0:T(8,128)(2,1)S(1)}, u32[]{:S(2)}, u32[]{:S(2)}) collective-permute-start(bf16[16,32,128]{2,1,0:T(8,128)(2,1)S(1)} %get-tuple-element.52), channel_id=1, source_target_pairs={{0,8},{2,10},{4,12},{6,14},{8,0},{10,2},{12,4},{14,6},{1,9},{3,11}... | collective-permute-start | bytes 393224 | tf_op jit(solution)/shard_map/ppermute | solution.py:492
  14.4 1.4 %collective-permute-start.5 = (bf16[16,32,128]{2,1,0:T(8,128)(2,1)S(1)}, bf16[16,32,128]{2,1,0:T(8,128)(2,1)S(1)}, u32[]{:S(2)}, u32[]{:S(2)}) collective-permute-start(bf16[16,32,128]{2,1,0:T(8,128)(2,1)S(1)} %get-tuple-element.53), channel_id=1, source_target_pairs={{0,10},{2,8},{4,14},{6,12},{8,2},{10,0},{12,6},{14,4},{1,11},{3,9}... | collective-permute-start | bytes 393224 | tf_op jit(solution)/shard_map/ppermute | solution.py:492
  15.8 0.3 collective-permute-start.6
  16.1 0.0 collective-permute-done.2.refs_0_
  16.1 3.6 %collective-permute-start.7 = (bf16[16,32,128]{2,1,0:T(8,128)(2,1)S(1)}, bf16[16,32,128]{2,1,0:T(8,128)(2,1)S(1)}, u32[]{:S(2)}, u32[]{:S(2)}) collective-permute-start(bf16[16,32,128]{2,1,0:T(8,128)(2,1)S(1)} %get-tuple-element.55), channel_id=1, source_target_pairs={{0,14},{2,12},{4,10},{6,8},{8,6},{10,4},{12,2},{14,0},{1,15},{3,13... | collective-permute-start | bytes 393224 | tf_op jit(solution)/shard_map/ppermute | solution.py:492
  19.7 0.0 collective-permute-done.3.refs_1_
  19.7 1.6 %collective-permute-start.8 = (bf16[16,32,128]{2,1,0:T(8,128)(2,1)S(1)}, bf16[16,32,128]{2,1,0:T(8,128)(2,1)S(1)}, u32[]{:S(2)}, u32[]{:S(2)}) collective-permute-start(bf16[16,32,128]{2,1,0:T(8,128)(2,1)S(1)} %get-tuple-element.56), channel_id=1, source_target_pairs={{0,12},{2,14},{4,6},{6,4},{8,10},{10,8},{12,0},{14,2},{1,13},{3,15... | collective-permute-start | bytes 393224 | tf_op jit(solution)/shard_map/ppermute | solution.py:492
  21.3 0.3 table.1.refs_8_
  21.6 3.3 %collective-permute-done.4.refs_2_ = bf16[16,32,128]{2,1,0:T(8,128)(2,1)S(1)} collective-permute-done((bf16[16,32,128]{2,1,0:T(8,128)(2,1)S(1)}, bf16[16,32,128]{2,1,0:T(8,128)(2,1)S(1)}, u32[]{:S(2)}, u32[]{:S(2)}) %collective-permute-start.4) | collective-permute-done | bytes 131104 | tf_op jit(solution)/shard_map/ppermute | solution.py:492
  24.9 9.0 %collective-permute-done.5.refs_3_ = bf16[16,32,128]{2,1,0:T(8,128)(2,1)S(1)} collective-permute-done((bf16[16,32,128]{2,1,0:T(8,128)(2,1)S(1)}, bf16[16,32,128]{2,1,0:T(8,128)(2,1)S(1)}, u32[]{:S(2)}, u32[]{:S(2)}) %collective-permute-start.5) | collective-permute-done | bytes 131104 | tf_op jit(solution)/shard_map/ppermute | solution.py:492
  33.9 0.0 collective-permute-done.6.refs_4_
  33.9 0.0 collective-permute-done.7.refs_5_
  33.9 0.0 collective-permute-done.8.refs_6_
  33.9 0.0 copy-done
  33.9 1.4 %peaks.1 = (f32[1,16]{1,0:T(1,128)}, f32[1,16]{1,0:T(1,128)}) custom-call(bf16[16,32,128]{2,1,0:T(8,128)(2,1)S(1)} %collective-permute-done.2.refs_0_, bf16[16,32,128]{2,1,0:T(8,128)(2,1)S(1)} %collective-permute-done.3.refs_1_, bf16[16,32,128]{2,1,0:T(8,128)(2,1)S(1)} %collective-permute-done.4.refs_2_, ...), custom_call_target="tpu_custom_call" | custom-call | tf_op jit(solution)/shard_map/peaks/pallas_call | solution.py:446
Async XLA Ops:
  4.0 2.3 %collective-permute-start.1 = (bf16[16,128,128]{2,1,0:T(8,128)(2,1)S(1)}, bf16[16,128,128]{2,1,0:T(8,128)(2,1)S(1)}, u32[]{:S(2)}, u32[]{:S(2)}) collective-permute-start(bf16[16,128,128]{2,1,0:T(8,128)(2,1)S(1)} %get-tuple-element.49), channel_id=1, source_target_pairs={{0,1},{1,0},{2,3},{3,2},{4,5},{5,4},{6,7},{7,6},{8,9},{9,8},{10,11... | collective-permute-start | bytes 1572872 | tf_op jit(solution)/shard_map/ppermute | solution.py:287
  5.3 2.0 %collective-permute-start = (bf16[16,128,128]{2,1,0:T(8,128)(2,1)S(1)}, bf16[16,128,128]{2,1,0:T(8,128)(2,1)S(1)}, u32[]{:S(2)}, u32[]{:S(2)}) collective-permute-start(bf16[16,128,128]{2,1,0:T(8,128)(2,1)S(1)} %get-tuple-element.48), channel_id=1, source_target_pairs={{0,1},{1,0},{2,3},{3,2},{4,5},{5,4},{6,7},{7,6},{8,9},{9,8},{10,11... | collective-permute-start | bytes 1572872 | tf_op jit(solution)/shard_map/ppermute | solution.py:291
  6.4 27.6 %copy-start = (f32[1,16]{1,0:T(1,128)S(1)}, f32[1,16]{1,0:T(1,128)}, u32[]{:S(2)}) copy-start(f32[1,16]{1,0:T(1,128)} %refs_9_.1) | copy-start | bytes 196
  7.6 8.6 %collective-permute-start.2 = (bf16[16,32,128]{2,1,0:T(8,128)(2,1)S(1)}, bf16[16,32,128]{2,1,0:T(8,128)(2,1)S(1)}, u32[]{:S(2)}, u32[]{:S(2)}) collective-permute-start(bf16[16,32,128]{2,1,0:T(8,128)(2,1)S(1)} %get-tuple-element.50), channel_id=1, source_target_pairs={{0,2},{2,0},{4,8},{6,10},{8,4},{10,6},{12,14},{14,12},{1,3},{3,1},... | collective-permute-start | bytes 393224 | tf_op jit(solution)/shard_map/ppermute | solution.py:492
  10.3 9.4 %collective-permute-start.3 = (bf16[16,32,128]{2,1,0:T(8,128)(2,1)S(1)}, bf16[16,32,128]{2,1,0:T(8,128)(2,1)S(1)}, u32[]{:S(2)}, u32[]{:S(2)}) collective-permute-start(bf16[16,32,128]{2,1,0:T(8,128)(2,1)S(1)} %get-tuple-element.51), channel_id=1, source_target_pairs={{0,4},{2,6},{4,0},{6,2},{8,12},{10,14},{12,8},{14,10},{1,5},{3,7},... | collective-permute-start | bytes 393224 | tf_op jit(solution)/shard_map/ppermute | solution.py:492
  11.9 13.0 %collective-permute-start.4 = (bf16[16,32,128]{2,1,0:T(8,128)(2,1)S(1)}, bf16[16,32,128]{2,1,0:T(8,128)(2,1)S(1)}, u32[]{:S(2)}, u32[]{:S(2)}) collective-permute-start(bf16[16,32,128]{2,1,0:T(8,128)(2,1)S(1)} %get-tuple-element.52), channel_id=1, source_target_pairs={{0,8},{2,10},{4,12},{6,14},{8,0},{10,2},{12,4},{14,6},{1,9},{3,11}... | collective-permute-start | bytes 393224 | tf_op jit(solution)/shard_map/ppermute | solution.py:492
  14.4 19.5 %collective-permute-start.5 = (bf16[16,32,128]{2,1,0:T(8,128)(2,1)S(1)}, bf16[16,32,128]{2,1,0:T(8,128)(2,1)S(1)}, u32[]{:S(2)}, u32[]{:S(2)}) collective-permute-start(bf16[16,32,128]{2,1,0:T(8,128)(2,1)S(1)} %get-tuple-element.53), channel_id=1, source_target_pairs={{0,10},{2,8},{4,14},{6,12},{8,2},{10,0},{12,6},{14,4},{1,11},{3,9}... | collective-permute-start | bytes 393224 | tf_op jit(solution)/shard_map/ppermute | solution.py:492
  15.8 18.1 %collective-permute-start.6 = (bf16[16,32,128]{2,1,0:T(8,128)(2,1)S(1)}, bf16[16,32,128]{2,1,0:T(8,128)(2,1)S(1)}, u32[]{:S(2)}, u32[]{:S(2)}) collective-permute-start(bf16[16,32,128]{2,1,0:T(8,128)(2,1)S(1)} %get-tuple-element.54), channel_id=1, source_target_pairs={{0,6},{2,4},{4,2},{6,0},{8,14},{10,12},{12,10},{14,8},{1,7},{3,5},... | collective-permute-start | bytes 393224 | tf_op jit(solution)/shard_map/ppermute | solution.py:492
  16.1 17.8 %collective-permute-start.7 = (bf16[16,32,128]{2,1,0:T(8,128)(2,1)S(1)}, bf16[16,32,128]{2,1,0:T(8,128)(2,1)S(1)}, u32[]{:S(2)}, u32[]{:S(2)}) collective-permute-start(bf16[16,32,128]{2,1,0:T(8,128)(2,1)S(1)} %get-tuple-element.55), channel_id=1, source_target_pairs={{0,14},{2,12},{4,10},{6,8},{8,6},{10,4},{12,2},{14,0},{1,15},{3,13... | collective-permute-start | bytes 393224 | tf_op jit(solution)/shard_map/ppermute | solution.py:492
  19.7 14.2 %collective-permute-start.8 = (bf16[16,32,128]{2,1,0:T(8,128)(2,1)S(1)}, bf16[16,32,128]{2,1,0:T(8,128)(2,1)S(1)}, u32[]{:S(2)}, u32[]{:S(2)}) collective-permute-start(bf16[16,32,128]{2,1,0:T(8,128)(2,1)S(1)} %get-tuple-element.56), channel_id=1, source_target_pairs={{0,12},{2,14},{4,6},{6,4},{8,10},{10,8},{12,0},{14,2},{1,13},{3,15... | collective-permute-start | bytes 393224 | tf_op jit(solution)/shard_map/ppermute | solution.py:492

commit v3 on v2

--- a/solution.py
+++ b/solution.py
@@ -14,6 +14,7 @@
 NB = 4
 SB = 32
 T_CAP = 1024
+TIME_BLOCK = 128
 
 EDGE = 0.6
 STEEP = 3.0
@@ -169,9 +170,10 @@
 
 def other_even_kernel(freq_total, slots, *refs):
     field_hbm, *small_hbm = refs[:7]
-    out_ref, own_picked_ref, field_ref, *kept = refs[7:25]
-    small, (field_sem, small_sem, *scratch) = refs[25:31], refs[31:]
-    delay_ref, channel_ref, blocks_ref, cells_ref, size_ref, slope_ref = small
+    out_ref, own_picked_ref, field_ref, size_ref, slope_ref, *kept = refs[7:20]
+    delay_ref, channel_ref, blocks_ref, cells_ref = refs[20:24]
+    field_sem, small_sem, *scratch = refs[24:]
+    small = (delay_ref, channel_ref, blocks_ref, cells_ref, size_ref, slope_ref)
     picked_ref, law_ref = scratch
     copies = [
         pltpu.make_async_copy(source, target, small_sem.at[i])
@@ -198,19 +200,12 @@
     picks = jnp.concatenate(
         [flaw_pick(slots, which, cells_ref) for which in groups], axis=0
     )
-    factors = [
-        kirchhoff(freq_total, slots, which, size_ref, slope_ref) for which in groups
-    ]
+    factors = kirchhoff(freq_total, slots, groups[0], size_ref, slope_ref)
     delays = delays_of(channel_ref, delay_ref, blocks_ref, groups, field_ref.shape[3])
-    laws = [
-        focal_base(freq_total, delays[:, i * ROWS : (i + 1) * ROWS]) for i in range(2)
-    ]
-    values = [picks]
-    for (even, step, odd), factor in zip(laws, factors):
-        values += [*even, *step, *odd, *factor]
-    for ref, value in zip(kept, [*values[:1], *values[3:]]):
+    even, step, odd = focal_base(freq_total, delays[:, :ROWS])
+    values = (picks, *step, *odd, *factors, delays[:, ROWS:])
+    for ref, value in zip(kept, values):
         ref[...] = value
-    even, step, _ = laws[0]
     store_law(law_ref, even, step)
 
     def wait(w):
@@ -218,7 +213,7 @@
             field_copies[w // part].wait()
 
     pick_fields(0, picks, field_ref, wait, (picked_ref, own_picked_ref))
-    store_spectra(0, picked_ref, law_ref, *factors[0], out_ref, 0)
+    store_spectra(0, picked_ref, law_ref, *factors, out_ref, 0)
     for copy in field_copies[2:]:
         copy.wait()
 
@@ -233,16 +228,16 @@
     store_spectra(1, picked_ref, law_ref, *k_refs, out_ref, 0)
 
 
-def own_kernel(*refs):
-    picked_refs, refs = refs[:2], refs[2:]
-    even, step, odd, k_refs = (refs[2 * i : 2 * i + 2] for i in range(4))
-    out_ref, law_ref = refs[8:]
-    step = [ref[...] for ref in step]
+def own_kernel(freq_total, slots, *refs):
+    picked_refs, (delays_ref, size_ref, slope_ref, out_ref, law_ref) = refs[:2], refs[2:]
+    even, step, odd = focal_base(freq_total, delays_ref[...])
     for parity, law in enumerate((even, odd)):
-        store_law(law_ref.at[parity], [ref[...] for ref in law], step)
+        store_law(law_ref.at[parity], law, step)
+    group = lax.axis_index("elem")
+    factors = kirchhoff(freq_total, slots, group, size_ref, slope_ref)
     for parity in range(2):
         store_spectra(
-            parity, picked_refs[parity], law_ref.at[parity], *k_refs, out_ref, parity * W_DEV
+            parity, picked_refs[parity], law_ref.at[parity], *factors, out_ref, parity * W_DEV
         )
 
 
@@ -270,32 +265,32 @@
     law = (W_HALF, 2 * elements, 2 * ROWS)
     base = [jax.ShapeDtypeStruct((elements, ROWS), jnp.float32)] * 2
     factors = [jax.ShapeDtypeStruct((FG, FG), jnp.float32)] * 2
-    kept = [jax.ShapeDtypeStruct((2 * FG, sites), jnp.bfloat16)]
-    kept += [*base, *base, *factors, *base, *base, *base, *factors]
+    kept = [jax.ShapeDtypeStruct((2 * FG, sites), jnp.bfloat16), *base, *base, *factors]
+    copied = [jax.ShapeDtypeStruct(a.shape, a.dtype) for a in (field, *small[4:])]
     work = [pltpu.VMEM(picked.shape, picked.dtype), pltpu.VMEM(law, jnp.bfloat16)]
-    even, even_picked, field, picks, *kept = call(
+    even, even_picked, field, size, slope, *kept, delays = call(
         functools.partial(other_even_kernel, freq_total, slots),
         "other_even",
         [hbm] * len(pinned),
-        [out, picked, jax.ShapeDtypeStruct(field.shape, field.dtype), *kept],
+        [out, picked, *copied, *kept, base[0]],
         [
             pltpu.SMEM(a.shape, a.dtype) if a.ndim == 1 else pltpu.VMEM(a.shape, a.dtype)
-            for a in small
+            for a in small[:4]
         ]
         + [pltpu.SemaphoreType.DMA((2, 2)), pltpu.SemaphoreType.DMA((len(small),)), *work],
     )(*pinned)
     even = lax.ppermute(even, "elem", swap)
     odd, odd_picked = call(
         other_odd_kernel, "other_odd", [vmem] * 8, [out, picked], work
-    )(field, picks, *kept[:6])
+    )(field, *kept)
     odd = lax.ppermute(odd, "elem", swap)
     (own,) = call(
-        own_kernel,
+        functools.partial(own_kernel, freq_total, slots),
         "own",
-        [vmem] * 10,
+        [vmem] * 5,
         [jax.ShapeDtypeStruct((2 * W_DEV, FG, ROWS), jnp.bfloat16)],
         [pltpu.VMEM((2, *law), jnp.bfloat16)],
-    )(even_picked, odd_picked, *kept[6:])
+    )(even_picked, odd_picked, delays, size, slope)
     return own, even, odd
 
 
@@ -331,42 +326,40 @@
 
 
 def table_kernel(freq_total, slots, table_ref):
-    height, depth = table_ref.shape[2:]
-    time_block = height // 2
-    row = lax.broadcasted_iota(jnp.int32, (height, depth // 2), 0)
-    column = lax.broadcasted_iota(jnp.int32, (height, depth // 2), 1)
-    out_imag = (row >= time_block).astype(jnp.int32)
-    time = pl.program_id(0) * time_block + row - out_imag * time_block
-    for parity in range(2):
-        freq = (column >> 1) * 2 + parity
-        if slots > 1:
-            lane = lax.broadcasted_iota(jnp.int32, (1, depth // 2), 1)
-            lane = (lane >> 1) * 2 + parity
-            freq = partner(slots, lane // W_DEV) * W_DEV + lane % W_DEV
-        steps = freq * time + ((column & 1) - out_imag) * (freq_total // 2)
-        steps = (steps + 2 * freq_total) & (2 * freq_total - 1)
-        _, value = sincos_turns(steps.astype(jnp.float32) * (0.5 / freq_total))
-        high = value.astype(jnp.bfloat16)
-        table_ref[0, parity, :, : depth // 2] = high
-        table_ref[0, parity, :, depth // 2 :] = (
-            value - high.astype(jnp.float32)
-        ).astype(jnp.bfloat16)
-
-
-def table(freq_total, slots, times, time_block):
-    blocks = times // time_block
-    shape = (blocks, 2, 2 * time_block, 2 * freq_total)
+    _, height, depth = table_ref.shape
+    time_block = TIME_BLOCK
+    row = lax.broadcasted_iota(jnp.int32, (height, depth), 0)
+    column = lax.broadcasted_iota(jnp.int32, (height, depth), 1)
+    out_imag = (row // time_block) % 2
+    time = pl.program_id(0) * time_block + row % time_block
+    later = row // (2 * time_block)
+    parity = (column >= depth // 2).astype(jnp.int32)
+    freq = ((column - parity * (depth // 2)) >> 1) * 2 + parity
+    if slots > 1:
+        lane = lax.broadcasted_iota(jnp.int32, (1, depth), 1)
+        odd = (lane >= depth // 2).astype(jnp.int32)
+        lane = ((lane - odd * (depth // 2)) >> 1) * 2 + odd
+        freq = partner(slots, lane // W_DEV) * W_DEV + lane % W_DEV
+    steps = freq * time + ((column & 1) - out_imag) * (freq_total // 2)
+    steps = (steps + (2 + later * freq) * freq_total) & (2 * freq_total - 1)
+    _, value = sincos_turns(steps.astype(jnp.float32) * (0.5 / freq_total))
+    table_ref[0] = value.astype(jnp.bfloat16)
+
+
+def table(freq_total, slots, times, folded):
+    blocks = times // TIME_BLOCK
+    shape = (blocks, (4 if folded else 2) * TIME_BLOCK, 2 * freq_total)
     return pl.pallas_call(
         functools.partial(table_kernel, freq_total, slots),
         grid=(blocks,),
-        out_specs=pl.BlockSpec((1, *shape[1:]), lambda i: (i, 0, 0, 0)),
+        out_specs=pl.BlockSpec((1, *shape[1:]), lambda i: (i, 0, 0)),
         out_shape=jax.ShapeDtypeStruct(shape, jnp.bfloat16),
         compiler_params=pltpu.CompilerParams(vmem_limit_bytes=VMEM_BYTES),
         name="table",
     )()
 
 
-def peak_kernel(freq_total, folded, sources, blocks, *refs):
+def peak_kernel(freq_total, sources, blocks, *refs):
     def first_step():
         return blocks == 1 or pl.program_id(0) == 0
 
@@ -376,7 +369,6 @@
     count = len(refs) - 5
     table_ref, noise_ref, peak_ref, found_ref, best_ref = refs[count:]
     columns = peak_ref.shape[1]
-    time_block = table_ref.shape[2] // 2
 
     @pl.when(first_step())
     def _():
@@ -384,30 +376,27 @@
 
     width = min(2, columns)
     for first in range(0, columns, width):
-        parts = []
-        for parity in range(2):
-            planes = slice(parity * W_DEV, (parity + 1) * W_DEV)
-            spectra = jnp.concatenate(
-                [
-                    jnp.concatenate(
-                        [
-                            refs[i][row + first + k, planes, :]
-                            for i, row in sources
-                        ]
-                        * 2,
-                        axis=0,
-                    )
-                    for k in range(width)
-                ],
-                axis=1,
-            )
-            parts.append(dot(table_ref[0, parity], spectra, ((1,), (0,))))
-        powers = []
-        for signal in [parts[0] + parts[1]] + [parts[0] - parts[1]] * folded:
-            real_part = signal[:time_block]
-            imag_part = signal[time_block:]
-            powers.append(real_part * real_part + imag_part * imag_part)
-        power = jnp.maximum(powers[0], powers[-1]) if folded else powers[0]
+        spectra = jnp.concatenate(
+            [
+                jnp.concatenate(
+                    [
+                        refs[i][row + first + k, plane : plane + W_DEV, :]
+                        for plane in (0, W_DEV)
+                        for i, row in sources
+                    ],
+                    axis=0,
+                )
+                for k in range(width)
+            ],
+            axis=1,
+        )
+        signal = dot(table_ref[0], spectra, ((1,), (0,)))
+        power = None
+        for top in range(0, signal.shape[0], 2 * TIME_BLOCK):
+            real_part = signal[top : top + TIME_BLOCK]
+            imag_part = signal[top + TIME_BLOCK : top + 2 * TIME_BLOCK]
+            value = real_part * real_part + imag_part * imag_part
+            power = value if power is None else jnp.maximum(power, value)
         power = jnp.max(power, axis=0, keepdims=True)
         for k in range(width):
             row = pl.ds(first + k, 1)
@@ -429,7 +418,7 @@
         found_ref[...] = 1.0 / (1.0 + jnp.exp(-score))
 
 
-def peaks(spectra, sources, twiddles, noise_level, freq_total, folded):
+def peaks(spectra, sources, twiddles, noise_level, freq_total):
     columns = noise_level.shape[1]
     blocks = twiddles.shape[0]
     if blocks == 1:
@@ -440,11 +429,11 @@
         out_spec = pl.BlockSpec((1, columns), lambda i: (0, 0))
         in_specs = [pl.BlockSpec(a.shape, lambda i: (0, 0, 0)) for a in spectra]
         in_specs += [
-            pl.BlockSpec((1, *twiddles.shape[1:]), lambda i: (i, 0, 0, 0)),
+            pl.BlockSpec((1, *twiddles.shape[1:]), lambda i: (i, 0, 0)),
             out_spec,
         ]
     return pl.pallas_call(
-        functools.partial(peak_kernel, freq_total, folded, sources, blocks),
+        functools.partial(peak_kernel, freq_total, sources, blocks),
         grid=grid,
         in_specs=in_specs,
         out_specs=[out_spec, out_spec],
@@ -481,7 +470,7 @@
     )
     folded = sample_count == 2 * freq_total
     times = sample_count // 2 if folded else sample_count
-    twiddles = table(freq_total, slots, times, min(128, times))
+    twiddles = table(freq_total, slots, times, folded)
     field = beam_field.reshape(W_HALF, 2, *beam_field.shape[1:])
     parts = add(*partials(field, small, swap, freq_total, slots), slots)
     if direct:
@@ -497,7 +486,7 @@
             lax.all_to_all(parts[0], "freq", split_axis=0, concat_axis=0, tiled=True)
         ]
         sources = [(0, s * (FG // freq_count)) for s in range(freq_count)]
-    return tuple(peaks(spectra, sources, twiddles, noise_level, freq_total, folded))
+    return tuple(peaks(spectra, sources, twiddles, noise_level, freq_total))
 
 
 def solution(mesh):

time: 35.5 us -> 35.3 us (level)
  waiting for transfers between devices: 12.9 us -> 12.2 us
  Pallas kernels: 7.38 us -> 7.89 us
  transfers between devices with their start and end apart: 9 -> 9, of which waited for: 3 -> 3; matrix products, arithmetic and copies ran while one was open for 0% -> 0% of each run, Pallas kernels for 7% -> 9%
where the time goes in v3:
time: 35.3 us; the launch traced here: 35.2 us
  starting transfers between devices  14.4 us (41%)
  waiting for transfers between devices  12.2 us (35%)
  Pallas kernels  7.89 us (22%)
  between operations  0.7 us (2%)
    ppermute x7, starting transfers between devices, body(): lax.ppermute(parts[slot], 'freq', pairs)  13.7 us
    ppermute x7, waiting for transfers between devices, body(): lax.ppermute(parts[slot], 'freq', pairs)  12 us
    pallas_call x1, Pallas kernels, partials(): call(functools.partial(other_even_kernel, freq_total, slots), 'other_even...  3.19 us
    pallas_call x1, Pallas kernels, peaks(): pl.pallas_call(functools.partial(peak_kernel, freq_total, sources, blocks...  1.36 us
    pallas_call x1, Pallas kernels, partials(): call(functools.partial(own_kernel, freq_total, slots), 'own', [vmem] * 5,...  1.32 us
    pallas_call x1, Pallas kernels, partials(): call(other_odd_kernel, 'other_odd', [vmem] * 8, [out, picked], work)  0.76 us
  transfers between devices with their start and end apart: 9, of which 3 were waited for; matrix products, arithmetic and copies ran while one was open for 0% of the time, Pallas kernels for 9%

profile of v3, /device:TPU:0, one launch (start us, length us, event | category | flops | bytes accessed | tf_op | source)
XLA Modules:
  0.0 35.2 jit_solution(9039779433983387874)
XLA Ops:
  0.6 3.2 %other_even.1 = (bf16[16,128,128]{2,1,0:T(8,128)(2,1)S(1)}, bf16[8,128,256]{2,1,0:T(8,128)(2,1)S(1)}, bf16[8,2,2,128,256]{4,3,2,1,0:T(8,128)(2,1)S(1)}, f32[2,12...) custom-call(bf16[8,2,2,128,256]{4,3,2,1,0:T(8,128)(2,1)} %bitcast.3,, ...), custom_call_target="tpu_custom_call" | custom-call | flops 1000 | bytes 1000 | tf_op jit(solution)/shard_map/other_even/pallas_call | solution.py:271
  3.8 0.5 %collective-permute-start.1 = (bf16[16,128,128]{2,1,0:T(8,128)(2,1)S(1)}, bf16[16,128,128]{2,1,0:T(8,128)(2,1)S(1)}, u32[]{:S(2)}, u32[]{:S(2)}) collective-permute-start(bf16[16,128,128]{2,1,0:T(8,128)(2,1)S(1)} %get-tuple-element.39), channel_id=1, source_target_pairs={{0,1},{1,0},{2,3},{3,2},{4,5},{5,4},{6,7},{7,6},{8,9},{9,8},{10,11... | collective-permute-start | bytes 1572872 | tf_op jit(solution)/shard_map/ppermute | solution.py:282
  4.3 0.8 %other_odd.1 = (bf16[16,128,128]{2,1,0:T(8,128)(2,1)S(1)}, bf16[8,128,256]{2,1,0:T(8,128)(2,1)S(1)}) custom-call(bf16[8,2,2,128,256]{4,3,2,1,0:T(8,128)(2,1)S(1)} %get-tuple-element.26.field_ref, bf16[256,256]{1,0:T(8,128)(2,1)S(1)} %get-tuple-element.27.picks_ref, f32[128,128]{1,0:T(8,128)S(1)} %get-tuple-element.28.refs_0_, ...), custom_call_target="tpu_custom_call" | custom-call | flops 1000 | bytes 1000 | tf_op jit(solution)/shard_map/other_odd/pallas_call | solution.py:283
  5.1 0.1 collective-permute-start
  5.2 1.3 %own.1.own_ref = bf16[32,128,128]{2,1,0:T(8,128)(2,1)S(1)} custom-call(bf16[8,128,256]{2,1,0:T(8,128)(2,1)S(1)} %get-tuple-element.25.refs_0_, bf16[8,128,256]{2,1,0:T(8,128)(2,1)S(1)} %get-tuple-element.34.refs_1_, f32[128,128]{1,0:T(8,128)S(1)} %get-tuple-element.35.refs_2_, f32[2,128]{1,0:T(2,128)S(1)} %get-tuple-element.36.refs_3_, ...), custom_call_target="tpu_custom_call" | custom-call | flops 1000 | bytes 1000 | tf_op jit(solution)/shard_map/own/pallas_call | solution.py:287
  6.6 0.0 copy-start
  6.6 0.0 collective-permute-done.1.even_ref
  6.6 0.3 add_even.1.held_ref
  6.9 0.2 collective-permute-done.odd_ref
  7.1 0.3 add_odd.1
  7.4 2.8 %collective-permute-start.2 = (bf16[16,32,128]{2,1,0:T(8,128)(2,1)S(1)}, bf16[16,32,128]{2,1,0:T(8,128)(2,1)S(1)}, u32[]{:S(2)}, u32[]{:S(2)}) collective-permute-start(bf16[16,32,128]{2,1,0:T(8,128)(2,1)S(1)} %get-tuple-element.40), channel_id=1, source_target_pairs={{0,2},{2,0},{4,8},{6,10},{8,4},{10,6},{12,14},{14,12},{1,3},{3,1},... | collective-permute-start | bytes 393224 | tf_op jit(solution)/shard_map/ppermute | solution.py:481
  10.3 1.6 %collective-permute-start.3 = (bf16[16,32,128]{2,1,0:T(8,128)(2,1)S(1)}, bf16[16,32,128]{2,1,0:T(8,128)(2,1)S(1)}, u32[]{:S(2)}, u32[]{:S(2)}) collective-permute-start(bf16[16,32,128]{2,1,0:T(8,128)(2,1)S(1)} %get-tuple-element.41), channel_id=1, source_target_pairs={{0,4},{2,6},{4,0},{6,2},{8,12},{10,14},{12,8},{14,10},{1,5},{3,7},... | collective-permute-start | bytes 393224 | tf_op jit(solution)/shard_map/ppermute | solution.py:481
  11.9 2.5 %collective-permute-start.4 = (bf16[16,32,128]{2,1,0:T(8,128)(2,1)S(1)}, bf16[16,32,128]{2,1,0:T(8,128)(2,1)S(1)}, u32[]{:S(2)}, u32[]{:S(2)}) collective-permute-start(bf16[16,32,128]{2,1,0:T(8,128)(2,1)S(1)} %get-tuple-element.42), channel_id=1, source_target_pairs={{0,8},{2,10},{4,12},{6,14},{8,0},{10,2},{12,4},{14,6},{1,9},{3,11}... | collective-permute-start | bytes 393224 | tf_op jit(solution)/shard_map/ppermute | solution.py:481
  14.4 1.3 %collective-permute-start.5 = (bf16[16,32,128]{2,1,0:T(8,128)(2,1)S(1)}, bf16[16,32,128]{2,1,0:T(8,128)(2,1)S(1)}, u32[]{:S(2)}, u32[]{:S(2)}) collective-permute-start(bf16[16,32,128]{2,1,0:T(8,128)(2,1)S(1)} %get-tuple-element.43), channel_id=1, source_target_pairs={{0,10},{2,8},{4,14},{6,12},{8,2},{10,0},{12,6},{14,4},{1,11},{3,9}... | collective-permute-start | bytes 393224 | tf_op jit(solution)/shard_map/ppermute | solution.py:481
  15.7 0.4 %collective-permute-start.6 = (bf16[16,32,128]{2,1,0:T(8,128)(2,1)S(1)}, bf16[16,32,128]{2,1,0:T(8,128)(2,1)S(1)}, u32[]{:S(2)}, u32[]{:S(2)}) collective-permute-start(bf16[16,32,128]{2,1,0:T(8,128)(2,1)S(1)} %get-tuple-element.44), channel_id=1, source_target_pairs={{0,6},{2,4},{4,2},{6,0},{8,14},{10,12},{12,10},{14,8},{1,7},{3,5},... | collective-permute-start | bytes 393224 | tf_op jit(solution)/shard_map/ppermute | solution.py:481
  16.1 0.0 collective-permute-done.2.refs_0_
  16.1 3.6 %collective-permute-start.7 = (bf16[16,32,128]{2,1,0:T(8,128)(2,1)S(1)}, bf16[16,32,128]{2,1,0:T(8,128)(2,1)S(1)}, u32[]{:S(2)}, u32[]{:S(2)}) collective-permute-start(bf16[16,32,128]{2,1,0:T(8,128)(2,1)S(1)} %get-tuple-element.45), channel_id=1, source_target_pairs={{0,14},{2,12},{4,10},{6,8},{8,6},{10,4},{12,2},{14,0},{1,15},{3,13... | collective-permute-start | bytes 393224 | tf_op jit(solution)/shard_map/ppermute | solution.py:481
  19.7 0.0 collective-permute-done.3.refs_1_
  19.7 1.5 %collective-permute-start.8 = (bf16[16,32,128]{2,1,0:T(8,128)(2,1)S(1)}, bf16[16,32,128]{2,1,0:T(8,128)(2,1)S(1)}, u32[]{:S(2)}, u32[]{:S(2)}) collective-permute-start(bf16[16,32,128]{2,1,0:T(8,128)(2,1)S(1)} %get-tuple-element.46), channel_id=1, source_target_pairs={{0,12},{2,14},{4,6},{6,4},{8,10},{10,8},{12,0},{14,2},{1,13},{3,15... | collective-permute-start | bytes 393224 | tf_op jit(solution)/shard_map/ppermute | solution.py:481
  21.2 0.6 %table.1.refs_8_ = bf16[1,512,256]{2,1,0:T(8,128)(2,1)S(1)} custom-call(), custom_call_target="tpu_custom_call" | custom-call | tf_op jit(solution)/shard_map/table/pallas_call | solution.py:352
  21.8 3.1 %collective-permute-done.4.refs_2_ = bf16[16,32,128]{2,1,0:T(8,128)(2,1)S(1)} collective-permute-done((bf16[16,32,128]{2,1,0:T(8,128)(2,1)S(1)}, bf16[16,32,128]{2,1,0:T(8,128)(2,1)S(1)}, u32[]{:S(2)}, u32[]{:S(2)}) %collective-permute-start.4) | collective-permute-done | bytes 131104 | tf_op jit(solution)/shard_map/ppermute | solution.py:481
  24.9 8.9 %collective-permute-done.5.refs_3_ = bf16[16,32,128]{2,1,0:T(8,128)(2,1)S(1)} collective-permute-done((bf16[16,32,128]{2,1,0:T(8,128)(2,1)S(1)}, bf16[16,32,128]{2,1,0:T(8,128)(2,1)S(1)}, u32[]{:S(2)}, u32[]{:S(2)}) %collective-permute-start.5) | collective-permute-done | bytes 131104 | tf_op jit(solution)/shard_map/ppermute | solution.py:481
  33.8 0.0 collective-permute-done.6.refs_4_
  33.8 0.0 collective-permute-done.7.refs_5_
  33.8 0.0 collective-permute-done.8.refs_6_
  33.8 0.0 copy-done
  33.8 1.4 %peaks.1 = (f32[1,16]{1,0:T(1,128)}, f32[1,16]{1,0:T(1,128)}) custom-call(bf16[16,32,128]{2,1,0:T(8,128)(2,1)S(1)} %collective-permute-done.2.refs_0_, bf16[16,32,128]{2,1,0:T(8,128)(2,1)S(1)} %collective-permute-done.3.refs_1_, bf16[16,32,128]{2,1,0:T(8,128)(2,1)S(1)} %collective-permute-done.4.refs_2_, ...), custom_call_target="tpu_custom_call" | custom-call | tf_op jit(solution)/shard_map/peaks/pallas_call | solution.py:435
Async XLA Ops:
  3.8 2.7 %collective-permute-start.1 = (bf16[16,128,128]{2,1,0:T(8,128)(2,1)S(1)}, bf16[16,128,128]{2,1,0:T(8,128)(2,1)S(1)}, u32[]{:S(2)}, u32[]{:S(2)}) collective-permute-start(bf16[16,128,128]{2,1,0:T(8,128)(2,1)S(1)} %get-tuple-element.39), channel_id=1, source_target_pairs={{0,1},{1,0},{2,3},{3,2},{4,5},{5,4},{6,7},{7,6},{8,9},{9,8},{10,11... | collective-permute-start | bytes 1572872 | tf_op jit(solution)/shard_map/ppermute | solution.py:282
  5.1 2.0 %collective-permute-start = (bf16[16,128,128]{2,1,0:T(8,128)(2,1)S(1)}, bf16[16,128,128]{2,1,0:T(8,128)(2,1)S(1)}, u32[]{:S(2)}, u32[]{:S(2)}) collective-permute-start(bf16[16,128,128]{2,1,0:T(8,128)(2,1)S(1)} %get-tuple-element.38), channel_id=1, source_target_pairs={{0,1},{1,0},{2,3},{3,2},{4,5},{5,4},{6,7},{7,6},{8,9},{9,8},{10,11... | collective-permute-start | bytes 1572872 | tf_op jit(solution)/shard_map/ppermute | solution.py:286
  6.6 27.2 %copy-start = (f32[1,16]{1,0:T(1,128)S(1)}, f32[1,16]{1,0:T(1,128)}, u32[]{:S(2)}) copy-start(f32[1,16]{1,0:T(1,128)} %refs_9_.1) | copy-start | bytes 196
  7.4 8.7 %collective-permute-start.2 = (bf16[16,32,128]{2,1,0:T(8,128)(2,1)S(1)}, bf16[16,32,128]{2,1,0:T(8,128)(2,1)S(1)}, u32[]{:S(2)}, u32[]{:S(2)}) collective-permute-start(bf16[16,32,128]{2,1,0:T(8,128)(2,1)S(1)} %get-tuple-element.40), channel_id=1, source_target_pairs={{0,2},{2,0},{4,8},{6,10},{8,4},{10,6},{12,14},{14,12},{1,3},{3,1},... | collective-permute-start | bytes 393224 | tf_op jit(solution)/shard_map/ppermute | solution.py:481
  10.3 9.4 %collective-permute-start.3 = (bf16[16,32,128]{2,1,0:T(8,128)(2,1)S(1)}, bf16[16,32,128]{2,1,0:T(8,128)(2,1)S(1)}, u32[]{:S(2)}, u32[]{:S(2)}) collective-permute-start(bf16[16,32,128]{2,1,0:T(8,128)(2,1)S(1)} %get-tuple-element.41), channel_id=1, source_target_pairs={{0,4},{2,6},{4,0},{6,2},{8,12},{10,14},{12,8},{14,10},{1,5},{3,7},... | collective-permute-start | bytes 393224 | tf_op jit(solution)/shard_map/ppermute | solution.py:481
  11.9 13.0 %collective-permute-start.4 = (bf16[16,32,128]{2,1,0:T(8,128)(2,1)S(1)}, bf16[16,32,128]{2,1,0:T(8,128)(2,1)S(1)}, u32[]{:S(2)}, u32[]{:S(2)}) collective-permute-start(bf16[16,32,128]{2,1,0:T(8,128)(2,1)S(1)} %get-tuple-element.42), channel_id=1, source_target_pairs={{0,8},{2,10},{4,12},{6,14},{8,0},{10,2},{12,4},{14,6},{1,9},{3,11}... | collective-permute-start | bytes 393224 | tf_op jit(solution)/shard_map/ppermute | solution.py:481
  14.4 19.4 %collective-permute-start.5 = (bf16[16,32,128]{2,1,0:T(8,128)(2,1)S(1)}, bf16[16,32,128]{2,1,0:T(8,128)(2,1)S(1)}, u32[]{:S(2)}, u32[]{:S(2)}) collective-permute-start(bf16[16,32,128]{2,1,0:T(8,128)(2,1)S(1)} %get-tuple-element.43), channel_id=1, source_target_pairs={{0,10},{2,8},{4,14},{6,12},{8,2},{10,0},{12,6},{14,4},{1,11},{3,9}... | collective-permute-start | bytes 393224 | tf_op jit(solution)/shard_map/ppermute | solution.py:481
  15.7 18.0 %collective-permute-start.6 = (bf16[16,32,128]{2,1,0:T(8,128)(2,1)S(1)}, bf16[16,32,128]{2,1,0:T(8,128)(2,1)S(1)}, u32[]{:S(2)}, u32[]{:S(2)}) collective-permute-start(bf16[16,32,128]{2,1,0:T(8,128)(2,1)S(1)} %get-tuple-element.44), channel_id=1, source_target_pairs={{0,6},{2,4},{4,2},{6,0},{8,14},{10,12},{12,10},{14,8},{1,7},{3,5},... | collective-permute-start | bytes 393224 | tf_op jit(solution)/shard_map/ppermute | solution.py:481
  16.1 17.7 %collective-permute-start.7 = (bf16[16,32,128]{2,1,0:T(8,128)(2,1)S(1)}, bf16[16,32,128]{2,1,0:T(8,128)(2,1)S(1)}, u32[]{:S(2)}, u32[]{:S(2)}) collective-permute-start(bf16[16,32,128]{2,1,0:T(8,128)(2,1)S(1)} %get-tuple-element.45), channel_id=1, source_target_pairs={{0,14},{2,12},{4,10},{6,8},{8,6},{10,4},{12,2},{14,0},{1,15},{3,13... | collective-permute-start | bytes 393224 | tf_op jit(solution)/shard_map/ppermute | solution.py:481
  19.7 14.1 %collective-permute-start.8 = (bf16[16,32,128]{2,1,0:T(8,128)(2,1)S(1)}, bf16[16,32,128]{2,1,0:T(8,128)(2,1)S(1)}, u32[]{:S(2)}, u32[]{:S(2)}) collective-permute-start(bf16[16,32,128]{2,1,0:T(8,128)(2,1)S(1)} %get-tuple-element.46), channel_id=1, source_target_pairs={{0,12},{2,14},{4,6},{6,4},{8,10},{10,8},{12,0},{14,2},{1,13},{3,15... | collective-permute-start | bytes 393224 | tf_op jit(solution)/shard_map/ppermute | solution.py:481

commit v4 on v2

--- a/solution.py
+++ b/solution.py
@@ -49,8 +49,11 @@
 
 def slot_masks(slots):
     half = slots // 2
-    between = (2, half, half + 1, 3, slots - 1)
-    return (0, 1, *between, slots - 2), (0, slots - 2, *between, 1)
+    between = (half, half + 1, 3)
+    return (
+        (0, 1, 2, slots - 2, *between, slots - 1),
+        (0, slots - 2, 2, slots - 1, *between, 1),
+    )
 
 
 def partner(slots, slot):
@@ -169,9 +172,10 @@
 
 def other_even_kernel(freq_total, slots, *refs):
     field_hbm, *small_hbm = refs[:7]
-    out_ref, own_picked_ref, field_ref, *kept = refs[7:25]
-    small, (field_sem, small_sem, *scratch) = refs[25:31], refs[31:]
-    delay_ref, channel_ref, blocks_ref, cells_ref, size_ref, slope_ref = small
+    out_ref, own_picked_ref, field_ref, size_ref, slope_ref, *kept = refs[7:20]
+    delay_ref, channel_ref, blocks_ref, cells_ref = refs[20:24]
+    field_sem, small_sem, *scratch = refs[24:]
+    small = (delay_ref, channel_ref, blocks_ref, cells_ref, size_ref, slope_ref)
     picked_ref, law_ref = scratch
     copies = [
         pltpu.make_async_copy(source, target, small_sem.at[i])
@@ -198,19 +202,12 @@
     picks = jnp.concatenate(
         [flaw_pick(slots, which, cells_ref) for which in groups], axis=0
     )
-    factors = [
-        kirchhoff(freq_total, slots, which, size_ref, slope_ref) for which in groups
-    ]
+    factors = kirchhoff(freq_total, slots, groups[0], size_ref, slope_ref)
     delays = delays_of(channel_ref, delay_ref, blocks_ref, groups, field_ref.shape[3])
-    laws = [
-        focal_base(freq_total, delays[:, i * ROWS : (i + 1) * ROWS]) for i in range(2)
-    ]
-    values = [picks]
-    for (even, step, odd), factor in zip(laws, factors):
-        values += [*even, *step, *odd, *factor]
-    for ref, value in zip(kept, [*values[:1], *values[3:]]):
+    even, step, odd = focal_base(freq_total, delays[:, :ROWS])
+    values = (picks, *step, *odd, *factors, delays[:, ROWS:])
+    for ref, value in zip(kept, values):
         ref[...] = value
-    even, step, _ = laws[0]
     store_law(law_ref, even, step)
 
     def wait(w):
@@ -218,7 +215,7 @@
             field_copies[w // part].wait()
 
     pick_fields(0, picks, field_ref, wait, (picked_ref, own_picked_ref))
-    store_spectra(0, picked_ref, law_ref, *factors[0], out_ref, 0)
+    store_spectra(0, picked_ref, law_ref, *factors, out_ref, 0)
     for copy in field_copies[2:]:
         copy.wait()
 
@@ -233,16 +230,16 @@
     store_spectra(1, picked_ref, law_ref, *k_refs, out_ref, 0)
 
 
-def own_kernel(*refs):
-    picked_refs, refs = refs[:2], refs[2:]
-    even, step, odd, k_refs = (refs[2 * i : 2 * i + 2] for i in range(4))
-    out_ref, law_ref = refs[8:]
-    step = [ref[...] for ref in step]
+def own_kernel(freq_total, slots, *refs):
+    picked_refs, (delays_ref, size_ref, slope_ref, out_ref, law_ref) = refs[:2], refs[2:]
+    even, step, odd = focal_base(freq_total, delays_ref[...])
     for parity, law in enumerate((even, odd)):
-        store_law(law_ref.at[parity], [ref[...] for ref in law], step)
+        store_law(law_ref.at[parity], law, step)
+    group = lax.axis_index("elem")
+    factors = kirchhoff(freq_total, slots, group, size_ref, slope_ref)
     for parity in range(2):
         store_spectra(
-            parity, picked_refs[parity], law_ref.at[parity], *k_refs, out_ref, parity * W_DEV
+            parity, picked_refs[parity], law_ref.at[parity], *factors, out_ref, parity * W_DEV
         )
 
 
@@ -270,32 +267,32 @@
     law = (W_HALF, 2 * elements, 2 * ROWS)
     base = [jax.ShapeDtypeStruct((elements, ROWS), jnp.float32)] * 2
     factors = [jax.ShapeDtypeStruct((FG, FG), jnp.float32)] * 2
-    kept = [jax.ShapeDtypeStruct((2 * FG, sites), jnp.bfloat16)]
-    kept += [*base, *base, *factors, *base, *base, *base, *factors]
+    kept = [jax.ShapeDtypeStruct((2 * FG, sites), jnp.bfloat16), *base, *base, *factors]
+    copied = [jax.ShapeDtypeStruct(a.shape, a.dtype) for a in (field, *small[4:])]
     work = [pltpu.VMEM(picked.shape, picked.dtype), pltpu.VMEM(law, jnp.bfloat16)]
-    even, even_picked, field, picks, *kept = call(
+    even, even_picked, field, size, slope, *kept, delays = call(
         functools.partial(other_even_kernel, freq_total, slots),
         "other_even",
         [hbm] * len(pinned),
-        [out, picked, jax.ShapeDtypeStruct(field.shape, field.dtype), *kept],
+        [out, picked, *copied, *kept, base[0]],
         [
             pltpu.SMEM(a.shape, a.dtype) if a.ndim == 1 else pltpu.VMEM(a.shape, a.dtype)
-            for a in small
+            for a in small[:4]
         ]
         + [pltpu.SemaphoreType.DMA((2, 2)), pltpu.SemaphoreType.DMA((len(small),)), *work],
     )(*pinned)
     even = lax.ppermute(even, "elem", swap)
     odd, odd_picked = call(
         other_odd_kernel, "other_odd", [vmem] * 8, [out, picked], work
-    )(field, picks, *kept[:6])
+    )(field, *kept)
     odd = lax.ppermute(odd, "elem", swap)
     (own,) = call(
-        own_kernel,
+        functools.partial(own_kernel, freq_total, slots),
         "own",
-        [vmem] * 10,
+        [vmem] * 5,
         [jax.ShapeDtypeStruct((2 * W_DEV, FG, ROWS), jnp.bfloat16)],
         [pltpu.VMEM((2, *law), jnp.bfloat16)],
-    )(even_picked, odd_picked, *kept[6:])
+    )(even_picked, odd_picked, delays, size, slope)
     return own, even, odd
 
 

time: 35.5 us -> 38 us (1.070)
  waiting for transfers between devices: 12.9 us -> 16.4 us
  starting transfers between devices: 14.4 us -> 13.1 us
    ppermute x7, waiting for transfers between devices: 12.3 us -> 16.2 us  [body(): lax.ppermute(parts[slot], 'freq', pairs)]
    ppermute x7, starting transfers between devices: 13.7 us -> 12.5 us  [body(): lax.ppermute(parts[slot], 'freq', pairs)]
  transfers between devices with their start and end apart: 9 -> 9, of which waited for: 3 -> 4; matrix products, arithmetic and copies ran while one was open for 0% -> 0% of each run, Pallas kernels for 7% -> 7%
where the time goes in v4:
time: 38 us; the launch traced here: 37.8 us
  waiting for transfers between devices  16.4 us (43%)
  starting transfers between devices  13.1 us (34%)
  Pallas kernels  7.57 us (20%)
  between operations  0.69 us (2%)
    ppermute x7, waiting for transfers between devices, body(): lax.ppermute(parts[slot], 'freq', pairs)  16.2 us
    ppermute x7, starting transfers between devices, body(): lax.ppermute(parts[slot], 'freq', pairs)  12.5 us
    pallas_call x1, Pallas kernels, partials(): call(functools.partial(other_even_kernel, freq_total, slots), 'other_even...  3.17 us
    pallas_call x1, Pallas kernels, peaks(): pl.pallas_call(functools.partial(peak_kernel, freq_total, folded, sources...  1.38 us
    pallas_call x1, Pallas kernels, partials(): call(functools.partial(own_kernel, freq_total, slots), 'own', [vmem] * 5,...  1.31 us
  transfers between devices with their start and end apart: 9, of which 4 were waited for; matrix products, arithmetic and copies ran while one was open for 0% of the time, Pallas kernels for 7%

profile of v4, /device:TPU:0, one launch (start us, length us, event | category | flops | bytes accessed | tf_op | source)
XLA Modules:
  0.0 37.8 jit_solution(4360720010217539403)
XLA Ops:
  0.6 3.2 %other_even.1 = (bf16[16,128,128]{2,1,0:T(8,128)(2,1)S(1)}, bf16[8,128,256]{2,1,0:T(8,128)(2,1)S(1)}, bf16[8,2,2,128,256]{4,3,2,1,0:T(8,128)(2,1)S(1)}, f32[2,12...) custom-call(bf16[8,2,2,128,256]{4,3,2,1,0:T(8,128)(2,1)} %bitcast.3,, ...), custom_call_target="tpu_custom_call" | custom-call | flops 1000 | bytes 1000 | tf_op jit(solution)/shard_map/other_even/pallas_call | solution.py:273
  3.8 0.5 %collective-permute-start.1 = (bf16[16,128,128]{2,1,0:T(8,128)(2,1)S(1)}, bf16[16,128,128]{2,1,0:T(8,128)(2,1)S(1)}, u32[]{:S(2)}, u32[]{:S(2)}) collective-permute-start(bf16[16,128,128]{2,1,0:T(8,128)(2,1)S(1)} %get-tuple-element.39), channel_id=1, source_target_pairs={{0,1},{1,0},{2,3},{3,2},{4,5},{5,4},{6,7},{7,6},{8,9},{9,8},{10,11... | collective-permute-start | bytes 1572872 | tf_op jit(solution)/shard_map/ppermute | solution.py:284
  4.3 0.8 %other_odd.1 = (bf16[16,128,128]{2,1,0:T(8,128)(2,1)S(1)}, bf16[8,128,256]{2,1,0:T(8,128)(2,1)S(1)}) custom-call(bf16[8,2,2,128,256]{4,3,2,1,0:T(8,128)(2,1)S(1)} %get-tuple-element.26.field_ref, bf16[256,256]{1,0:T(8,128)(2,1)S(1)} %get-tuple-element.27.picks_ref, f32[128,128]{1,0:T(8,128)S(1)} %get-tuple-element.28.refs_0_, ...), custom_call_target="tpu_custom_call" | custom-call | flops 1000 | bytes 1000 | tf_op jit(solution)/shard_map/other_odd/pallas_call | solution.py:285
  5.1 0.1 collective-permute-start
  5.2 1.3 %own.1.own_ref = bf16[32,128,128]{2,1,0:T(8,128)(2,1)S(1)} custom-call(bf16[8,128,256]{2,1,0:T(8,128)(2,1)S(1)} %get-tuple-element.25.refs_0_, bf16[8,128,256]{2,1,0:T(8,128)(2,1)S(1)} %get-tuple-element.34.refs_1_, f32[128,128]{1,0:T(8,128)S(1)} %get-tuple-element.35.refs_2_, f32[2,128]{1,0:T(2,128)S(1)} %get-tuple-element.36.refs_3_, ...), custom_call_target="tpu_custom_call" | custom-call | flops 1000 | bytes 1000 | tf_op jit(solution)/shard_map/own/pallas_call | solution.py:289
  6.5 0.0 copy-start
  6.5 0.0 collective-permute-done.1.even_ref
  6.6 0.3 add_even.1.held_ref
  6.9 0.2 collective-permute-done.odd_ref
  7.1 0.3 add_odd.1
  7.4 2.8 %collective-permute-start.2 = (bf16[16,32,128]{2,1,0:T(8,128)(2,1)S(1)}, bf16[16,32,128]{2,1,0:T(8,128)(2,1)S(1)}, u32[]{:S(2)}, u32[]{:S(2)}) collective-permute-start(bf16[16,32,128]{2,1,0:T(8,128)(2,1)S(1)} %get-tuple-element.40), channel_id=1, source_target_pairs={{0,2},{2,0},{4,8},{6,10},{8,4},{10,6},{12,14},{14,12},{1,3},{3,1},... | collective-permute-start | bytes 393224 | tf_op jit(solution)/shard_map/ppermute | solution.py:489
  10.2 1.6 %collective-permute-start.3 = (bf16[16,32,128]{2,1,0:T(8,128)(2,1)S(1)}, bf16[16,32,128]{2,1,0:T(8,128)(2,1)S(1)}, u32[]{:S(2)}, u32[]{:S(2)}) collective-permute-start(bf16[16,32,128]{2,1,0:T(8,128)(2,1)S(1)} %get-tuple-element.41), channel_id=1, source_target_pairs={{0,4},{2,6},{4,0},{6,2},{8,12},{10,14},{12,8},{14,10},{1,5},{3,7},... | collective-permute-start | bytes 393224 | tf_op jit(solution)/shard_map/ppermute | solution.py:489
  11.9 2.0 %collective-permute-start.4 = (bf16[16,32,128]{2,1,0:T(8,128)(2,1)S(1)}, bf16[16,32,128]{2,1,0:T(8,128)(2,1)S(1)}, u32[]{:S(2)}, u32[]{:S(2)}) collective-permute-start(bf16[16,32,128]{2,1,0:T(8,128)(2,1)S(1)} %get-tuple-element.42), channel_id=1, source_target_pairs={{0,12},{2,14},{4,10},{6,8},{8,6},{10,4},{12,0},{14,2},{1,13},{3,15... | collective-permute-start | bytes 393224 | tf_op jit(solution)/shard_map/ppermute | solution.py:489
  13.8 0.6 %collective-permute-start.5 = (bf16[16,32,128]{2,1,0:T(8,128)(2,1)S(1)}, bf16[16,32,128]{2,1,0:T(8,128)(2,1)S(1)}, u32[]{:S(2)}, u32[]{:S(2)}) collective-permute-start(bf16[16,32,128]{2,1,0:T(8,128)(2,1)S(1)} %get-tuple-element.43), channel_id=1, source_target_pairs={{0,8},{2,10},{4,12},{6,14},{8,0},{10,2},{12,4},{14,6},{1,9},{3,11}... | collective-permute-start | bytes 393224 | tf_op jit(solution)/shard_map/ppermute | solution.py:489
  14.4 2.7 %collective-permute-start.6 = (bf16[16,32,128]{2,1,0:T(8,128)(2,1)S(1)}, bf16[16,32,128]{2,1,0:T(8,128)(2,1)S(1)}, u32[]{:S(2)}, u32[]{:S(2)}) collective-permute-start(bf16[16,32,128]{2,1,0:T(8,128)(2,1)S(1)} %get-tuple-element.44), channel_id=1, source_target_pairs={{0,10},{2,8},{4,14},{6,12},{8,2},{10,0},{12,6},{14,4},{1,11},{3,9}... | collective-permute-start | bytes 393224 | tf_op jit(solution)/shard_map/ppermute | solution.py:489
  17.1 0.0 collective-permute-done.2.refs_0_
  17.1 1.7 %collective-permute-start.7 = (bf16[16,32,128]{2,1,0:T(8,128)(2,1)S(1)}, bf16[16,32,128]{2,1,0:T(8,128)(2,1)S(1)}, u32[]{:S(2)}, u32[]{:S(2)}) collective-permute-start(bf16[16,32,128]{2,1,0:T(8,128)(2,1)S(1)} %get-tuple-element.45), channel_id=1, source_target_pairs={{0,6},{2,4},{4,2},{6,0},{8,14},{10,12},{12,10},{14,8},{1,7},{3,5},... | collective-permute-start | bytes 393224 | tf_op jit(solution)/shard_map/ppermute | solution.py:489
  18.8 0.0 collective-permute-done.3.refs_1_
  18.8 1.2 %collective-permute-start.8 = (bf16[16,32,128]{2,1,0:T(8,128)(2,1)S(1)}, bf16[16,32,128]{2,1,0:T(8,128)(2,1)S(1)}, u32[]{:S(2)}, u32[]{:S(2)}) collective-permute-start(bf16[16,32,128]{2,1,0:T(8,128)(2,1)S(1)} %get-tuple-element.46), channel_id=1, source_target_pairs={{0,14},{2,12},{4,6},{6,4},{8,10},{10,8},{12,2},{14,0},{1,15},{3,13... | collective-permute-start | bytes 393224 | tf_op jit(solution)/shard_map/ppermute | solution.py:489
  19.9 0.3 table.1.refs_8_
  20.2 0.8 %collective-permute-done.4.refs_2_ = bf16[16,32,128]{2,1,0:T(8,128)(2,1)S(1)} collective-permute-done((bf16[16,32,128]{2,1,0:T(8,128)(2,1)S(1)}, bf16[16,32,128]{2,1,0:T(8,128)(2,1)S(1)}, u32[]{:S(2)}, u32[]{:S(2)}) %collective-permute-start.4) | collective-permute-done | bytes 131104 | tf_op jit(solution)/shard_map/ppermute | solution.py:489
  21.0 12.2 %collective-permute-done.5.refs_3_ = bf16[16,32,128]{2,1,0:T(8,128)(2,1)S(1)} collective-permute-done((bf16[16,32,128]{2,1,0:T(8,128)(2,1)S(1)}, bf16[16,32,128]{2,1,0:T(8,128)(2,1)S(1)}, u32[]{:S(2)}, u32[]{:S(2)}) %collective-permute-start.5) | collective-permute-done | bytes 131104 | tf_op jit(solution)/shard_map/ppermute | solution.py:489
  33.3 3.2 %collective-permute-done.6.refs_4_ = bf16[16,32,128]{2,1,0:T(8,128)(2,1)S(1)} collective-permute-done((bf16[16,32,128]{2,1,0:T(8,128)(2,1)S(1)}, bf16[16,32,128]{2,1,0:T(8,128)(2,1)S(1)}, u32[]{:S(2)}, u32[]{:S(2)}) %collective-permute-start.6) | collective-permute-done | bytes 131104 | tf_op jit(solution)/shard_map/ppermute | solution.py:489
  36.5 0.0 collective-permute-done.7.refs_5_
  36.5 0.0 collective-permute-done.8.refs_6_
  36.5 0.0 copy-done
  36.5 1.4 %peaks.1 = (f32[1,16]{1,0:T(1,128)}, f32[1,16]{1,0:T(1,128)}) custom-call(bf16[16,32,128]{2,1,0:T(8,128)(2,1)S(1)} %collective-permute-done.2.refs_0_, bf16[16,32,128]{2,1,0:T(8,128)(2,1)S(1)} %collective-permute-done.3.refs_1_, bf16[16,32,128]{2,1,0:T(8,128)(2,1)S(1)} %collective-permute-done.4.refs_2_, ...), custom_call_target="tpu_custom_call" | custom-call | tf_op jit(solution)/shard_map/peaks/pallas_call | solution.py:443
Async XLA Ops:
  3.8 2.7 %collective-permute-start.1 = (bf16[16,128,128]{2,1,0:T(8,128)(2,1)S(1)}, bf16[16,128,128]{2,1,0:T(8,128)(2,1)S(1)}, u32[]{:S(2)}, u32[]{:S(2)}) collective-permute-start(bf16[16,128,128]{2,1,0:T(8,128)(2,1)S(1)} %get-tuple-element.39), channel_id=1, source_target_pairs={{0,1},{1,0},{2,3},{3,2},{4,5},{5,4},{6,7},{7,6},{8,9},{9,8},{10,11... | collective-permute-start | bytes 1572872 | tf_op jit(solution)/shard_map/ppermute | solution.py:284
  5.1 2.0 %collective-permute-start = (bf16[16,128,128]{2,1,0:T(8,128)(2,1)S(1)}, bf16[16,128,128]{2,1,0:T(8,128)(2,1)S(1)}, u32[]{:S(2)}, u32[]{:S(2)}) collective-permute-start(bf16[16,128,128]{2,1,0:T(8,128)(2,1)S(1)} %get-tuple-element.38), channel_id=1, source_target_pairs={{0,1},{1,0},{2,3},{3,2},{4,5},{5,4},{6,7},{7,6},{8,9},{9,8},{10,11... | collective-permute-start | bytes 1572872 | tf_op jit(solution)/shard_map/ppermute | solution.py:288
  6.5 29.9 %copy-start = (f32[1,16]{1,0:T(1,128)S(1)}, f32[1,16]{1,0:T(1,128)}, u32[]{:S(2)}) copy-start(f32[1,16]{1,0:T(1,128)} %refs_9_.1) | copy-start | bytes 196
  7.4 9.7 %collective-permute-start.2 = (bf16[16,32,128]{2,1,0:T(8,128)(2,1)S(1)}, bf16[16,32,128]{2,1,0:T(8,128)(2,1)S(1)}, u32[]{:S(2)}, u32[]{:S(2)}) collective-permute-start(bf16[16,32,128]{2,1,0:T(8,128)(2,1)S(1)} %get-tuple-element.40), channel_id=1, source_target_pairs={{0,2},{2,0},{4,8},{6,10},{8,4},{10,6},{12,14},{14,12},{1,3},{3,1},... | collective-permute-start | bytes 393224 | tf_op jit(solution)/shard_map/ppermute | solution.py:489
  10.2 8.5 %collective-permute-start.3 = (bf16[16,32,128]{2,1,0:T(8,128)(2,1)S(1)}, bf16[16,32,128]{2,1,0:T(8,128)(2,1)S(1)}, u32[]{:S(2)}, u32[]{:S(2)}) collective-permute-start(bf16[16,32,128]{2,1,0:T(8,128)(2,1)S(1)} %get-tuple-element.41), channel_id=1, source_target_pairs={{0,4},{2,6},{4,0},{6,2},{8,12},{10,14},{12,8},{14,10},{1,5},{3,7},... | collective-permute-start | bytes 393224 | tf_op jit(solution)/shard_map/ppermute | solution.py:489
  11.9 9.2 %collective-permute-start.4 = (bf16[16,32,128]{2,1,0:T(8,128)(2,1)S(1)}, bf16[16,32,128]{2,1,0:T(8,128)(2,1)S(1)}, u32[]{:S(2)}, u32[]{:S(2)}) collective-permute-start(bf16[16,32,128]{2,1,0:T(8,128)(2,1)S(1)} %get-tuple-element.42), channel_id=1, source_target_pairs={{0,12},{2,14},{4,10},{6,8},{8,6},{10,4},{12,0},{14,2},{1,13},{3,15... | collective-permute-start | bytes 393224 | tf_op jit(solution)/shard_map/ppermute | solution.py:489
  13.8 19.4 %collective-permute-start.5 = (bf16[16,32,128]{2,1,0:T(8,128)(2,1)S(1)}, bf16[16,32,128]{2,1,0:T(8,128)(2,1)S(1)}, u32[]{:S(2)}, u32[]{:S(2)}) collective-permute-start(bf16[16,32,128]{2,1,0:T(8,128)(2,1)S(1)} %get-tuple-element.43), channel_id=1, source_target_pairs={{0,8},{2,10},{4,12},{6,14},{8,0},{10,2},{12,4},{14,6},{1,9},{3,11}... | collective-permute-start | bytes 393224 | tf_op jit(solution)/shard_map/ppermute | solution.py:489
  14.4 22.1 %collective-permute-start.6 = (bf16[16,32,128]{2,1,0:T(8,128)(2,1)S(1)}, bf16[16,32,128]{2,1,0:T(8,128)(2,1)S(1)}, u32[]{:S(2)}, u32[]{:S(2)}) collective-permute-start(bf16[16,32,128]{2,1,0:T(8,128)(2,1)S(1)} %get-tuple-element.44), channel_id=1, source_target_pairs={{0,10},{2,8},{4,14},{6,12},{8,2},{10,0},{12,6},{14,4},{1,11},{3,9}... | collective-permute-start | bytes 393224 | tf_op jit(solution)/shard_map/ppermute | solution.py:489
  17.1 19.4 %collective-permute-start.7 = (bf16[16,32,128]{2,1,0:T(8,128)(2,1)S(1)}, bf16[16,32,128]{2,1,0:T(8,128)(2,1)S(1)}, u32[]{:S(2)}, u32[]{:S(2)}) collective-permute-start(bf16[16,32,128]{2,1,0:T(8,128)(2,1)S(1)} %get-tuple-element.45), channel_id=1, source_target_pairs={{0,6},{2,4},{4,2},{6,0},{8,14},{10,12},{12,10},{14,8},{1,7},{3,5},... | collective-permute-start | bytes 393224 | tf_op jit(solution)/shard_map/ppermute | solution.py:489
  18.8 17.7 %collective-permute-start.8 = (bf16[16,32,128]{2,1,0:T(8,128)(2,1)S(1)}, bf16[16,32,128]{2,1,0:T(8,128)(2,1)S(1)}, u32[]{:S(2)}, u32[]{:S(2)}) collective-permute-start(bf16[16,32,128]{2,1,0:T(8,128)(2,1)S(1)} %get-tuple-element.46), channel_id=1, source_target_pairs={{0,14},{2,12},{4,6},{6,4},{8,10},{10,8},{12,2},{14,0},{1,15},{3,13... | collective-permute-start | bytes 393224 | tf_op jit(solution)/shard_map/ppermute | solution.py:489

commit v5 on v4

--- a/solution.py
+++ b/solution.py
@@ -49,11 +49,8 @@
 
 def slot_masks(slots):
     half = slots // 2
-    between = (half, half + 1, 3)
-    return (
-        (0, 1, 2, slots - 2, *between, slots - 1),
-        (0, slots - 2, 2, slots - 1, *between, 1),
-    )
+    between = (2, half, half + 1, slots - 1, 3)
+    return (0, 1, *between, slots - 2), (0, slots - 2, *between, 1)
 
 
 def partner(slots, slot):

time: 38 us -> 35.4 us (0.932)
  waiting for transfers between devices: 16.4 us -> 13.1 us
  starting transfers between devices: 13.1 us -> 13.8 us
    ppermute x7, waiting for transfers between devices: 16.2 us -> 13 us  [body(): lax.ppermute(parts[slot], 'freq', pairs)]
    ppermute x7, starting transfers between devices: 12.5 us -> 13.2 us  [body(): lax.ppermute(parts[slot], 'freq', pairs)]
  transfers between devices with their start and end apart: 9 -> 9, of which waited for: 4 -> 3; matrix products, arithmetic and copies ran while one was open for 0% -> 0% of each run, Pallas kernels for 7% -> 8%
where the time goes in v5:
time: 35.4 us; the launch traced here: 35.2 us
  starting transfers between devices  13.8 us (39%)
  waiting for transfers between devices  13.1 us (37%)
  Pallas kernels  7.59 us (21%)
  between operations  0.7 us (2%)
    ppermute x7, starting transfers between devices, body(): lax.ppermute(parts[slot], 'freq', pairs)  13.2 us
    ppermute x7, waiting for transfers between devices, body(): lax.ppermute(parts[slot], 'freq', pairs)  13 us
    pallas_call x1, Pallas kernels, partials(): call(functools.partial(other_even_kernel, freq_total, slots), 'other_even...  3.19 us
    pallas_call x1, Pallas kernels, peaks(): pl.pallas_call(functools.partial(peak_kernel, freq_total, folded, sources...  1.38 us
    pallas_call x1, Pallas kernels, partials(): call(functools.partial(own_kernel, freq_total, slots), 'own', [vmem] * 5,...  1.32 us
    pallas_call x1, Pallas kernels, partials(): call(other_odd_kernel, 'other_odd', [vmem] * 8, [out, picked], work)  0.76 us
  transfers between devices with their start and end apart: 9, of which 3 were waited for; matrix products, arithmetic and copies ran while one was open for 0% of the time, Pallas kernels for 8%

profile of v5, /device:TPU:0, one launch (start us, length us, event | category | flops | bytes accessed | tf_op | source)
XLA Modules:
  0.0 35.2 jit_solution(8276863020210662541)
XLA Ops:
  0.6 3.2 %other_even.1 = (bf16[16,128,128]{2,1,0:T(8,128)(2,1)S(1)}, bf16[8,128,256]{2,1,0:T(8,128)(2,1)S(1)}, bf16[8,2,2,128,256]{4,3,2,1,0:T(8,128)(2,1)S(1)}, f32[2,12...) custom-call(bf16[8,2,2,128,256]{4,3,2,1,0:T(8,128)(2,1)} %bitcast.3,, ...), custom_call_target="tpu_custom_call" | custom-call | flops 1000 | bytes 1000 | tf_op jit(solution)/shard_map/other_even/pallas_call | solution.py:270
  3.8 0.5 %collective-permute-start.1 = (bf16[16,128,128]{2,1,0:T(8,128)(2,1)S(1)}, bf16[16,128,128]{2,1,0:T(8,128)(2,1)S(1)}, u32[]{:S(2)}, u32[]{:S(2)}) collective-permute-start(bf16[16,128,128]{2,1,0:T(8,128)(2,1)S(1)} %get-tuple-element.39), channel_id=1, source_target_pairs={{0,1},{1,0},{2,3},{3,2},{4,5},{5,4},{6,7},{7,6},{8,9},{9,8},{10,11... | collective-permute-start | bytes 1572872 | tf_op jit(solution)/shard_map/ppermute | solution.py:281
  4.3 0.8 %other_odd.1 = (bf16[16,128,128]{2,1,0:T(8,128)(2,1)S(1)}, bf16[8,128,256]{2,1,0:T(8,128)(2,1)S(1)}) custom-call(bf16[8,2,2,128,256]{4,3,2,1,0:T(8,128)(2,1)S(1)} %get-tuple-element.26.field_ref, bf16[256,256]{1,0:T(8,128)(2,1)S(1)} %get-tuple-element.27.picks_ref, f32[128,128]{1,0:T(8,128)S(1)} %get-tuple-element.28.refs_0_, ...), custom_call_target="tpu_custom_call" | custom-call | flops 1000 | bytes 1000 | tf_op jit(solution)/shard_map/other_odd/pallas_call | solution.py:282
  5.1 0.1 collective-permute-start
  5.2 1.3 %own.1.own_ref = bf16[32,128,128]{2,1,0:T(8,128)(2,1)S(1)} custom-call(bf16[8,128,256]{2,1,0:T(8,128)(2,1)S(1)} %get-tuple-element.25.refs_0_, bf16[8,128,256]{2,1,0:T(8,128)(2,1)S(1)} %get-tuple-element.34.refs_1_, f32[128,128]{1,0:T(8,128)S(1)} %get-tuple-element.35.refs_2_, f32[2,128]{1,0:T(2,128)S(1)} %get-tuple-element.36.refs_3_, ...), custom_call_target="tpu_custom_call" | custom-call | flops 1000 | bytes 1000 | tf_op jit(solution)/shard_map/own/pallas_call | solution.py:286
  6.6 0.0 copy-start
  6.6 0.0 collective-permute-done.1.even_ref
  6.6 0.3 add_even.1.held_ref
  6.9 0.2 collective-permute-done.odd_ref
  7.1 0.3 add_odd.1
  7.4 2.8 %collective-permute-start.2 = (bf16[16,32,128]{2,1,0:T(8,128)(2,1)S(1)}, bf16[16,32,128]{2,1,0:T(8,128)(2,1)S(1)}, u32[]{:S(2)}, u32[]{:S(2)}) collective-permute-start(bf16[16,32,128]{2,1,0:T(8,128)(2,1)S(1)} %get-tuple-element.40), channel_id=1, source_target_pairs={{0,2},{2,0},{4,8},{6,10},{8,4},{10,6},{12,14},{14,12},{1,3},{3,1},... | collective-permute-start | bytes 393224 | tf_op jit(solution)/shard_map/ppermute | solution.py:486
  10.3 1.6 %collective-permute-start.3 = (bf16[16,32,128]{2,1,0:T(8,128)(2,1)S(1)}, bf16[16,32,128]{2,1,0:T(8,128)(2,1)S(1)}, u32[]{:S(2)}, u32[]{:S(2)}) collective-permute-start(bf16[16,32,128]{2,1,0:T(8,128)(2,1)S(1)} %get-tuple-element.41), channel_id=1, source_target_pairs={{0,4},{2,6},{4,0},{6,2},{8,12},{10,14},{12,8},{14,10},{1,5},{3,7},... | collective-permute-start | bytes 393224 | tf_op jit(solution)/shard_map/ppermute | solution.py:486
  11.9 2.5 %collective-permute-start.4 = (bf16[16,32,128]{2,1,0:T(8,128)(2,1)S(1)}, bf16[16,32,128]{2,1,0:T(8,128)(2,1)S(1)}, u32[]{:S(2)}, u32[]{:S(2)}) collective-permute-start(bf16[16,32,128]{2,1,0:T(8,128)(2,1)S(1)} %get-tuple-element.42), channel_id=1, source_target_pairs={{0,8},{2,10},{4,12},{6,14},{8,0},{10,2},{12,4},{14,6},{1,9},{3,11}... | collective-permute-start | bytes 393224 | tf_op jit(solution)/shard_map/ppermute | solution.py:486
  14.4 1.3 %collective-permute-start.5 = (bf16[16,32,128]{2,1,0:T(8,128)(2,1)S(1)}, bf16[16,32,128]{2,1,0:T(8,128)(2,1)S(1)}, u32[]{:S(2)}, u32[]{:S(2)}) collective-permute-start(bf16[16,32,128]{2,1,0:T(8,128)(2,1)S(1)} %get-tuple-element.43), channel_id=1, source_target_pairs={{0,10},{2,8},{4,14},{6,12},{8,2},{10,0},{12,6},{14,4},{1,11},{3,9}... | collective-permute-start | bytes 393224 | tf_op jit(solution)/shard_map/ppermute | solution.py:486
  15.7 1.9 %collective-permute-start.6 = (bf16[16,32,128]{2,1,0:T(8,128)(2,1)S(1)}, bf16[16,32,128]{2,1,0:T(8,128)(2,1)S(1)}, u32[]{:S(2)}, u32[]{:S(2)}) collective-permute-start(bf16[16,32,128]{2,1,0:T(8,128)(2,1)S(1)} %get-tuple-element.44), channel_id=1, source_target_pairs={{0,14},{2,12},{4,10},{6,8},{8,6},{10,4},{12,2},{14,0},{1,15},{3,13... | collective-permute-start | bytes 393224 | tf_op jit(solution)/shard_map/ppermute | solution.py:486
  17.7 0.0 collective-permute-done.2.refs_0_
  17.7 1.1 %collective-permute-start.7 = (bf16[16,32,128]{2,1,0:T(8,128)(2,1)S(1)}, bf16[16,32,128]{2,1,0:T(8,128)(2,1)S(1)}, u32[]{:S(2)}, u32[]{:S(2)}) collective-permute-start(bf16[16,32,128]{2,1,0:T(8,128)(2,1)S(1)} %get-tuple-element.45), channel_id=1, source_target_pairs={{0,6},{2,4},{4,2},{6,0},{8,14},{10,12},{12,10},{14,8},{1,7},{3,5},... | collective-permute-start | bytes 393224 | tf_op jit(solution)/shard_map/ppermute | solution.py:486
  18.8 0.0 collective-permute-done.3.refs_1_
  18.8 1.8 %collective-permute-start.8 = (bf16[16,32,128]{2,1,0:T(8,128)(2,1)S(1)}, bf16[16,32,128]{2,1,0:T(8,128)(2,1)S(1)}, u32[]{:S(2)}, u32[]{:S(2)}) collective-permute-start(bf16[16,32,128]{2,1,0:T(8,128)(2,1)S(1)} %get-tuple-element.46), channel_id=1, source_target_pairs={{0,12},{2,14},{4,6},{6,4},{8,10},{10,8},{12,0},{14,2},{1,13},{3,15... | collective-permute-start | bytes 393224 | tf_op jit(solution)/shard_map/ppermute | solution.py:486
  20.6 0.3 table.1.refs_8_
  20.9 6.8 %collective-permute-done.4.refs_2_ = bf16[16,32,128]{2,1,0:T(8,128)(2,1)S(1)} collective-permute-done((bf16[16,32,128]{2,1,0:T(8,128)(2,1)S(1)}, bf16[16,32,128]{2,1,0:T(8,128)(2,1)S(1)}, u32[]{:S(2)}, u32[]{:S(2)}) %collective-permute-start.4) | collective-permute-done | bytes 131104 | tf_op jit(solution)/shard_map/ppermute | solution.py:486
  27.7 6.2 %collective-permute-done.5.refs_3_ = bf16[16,32,128]{2,1,0:T(8,128)(2,1)S(1)} collective-permute-done((bf16[16,32,128]{2,1,0:T(8,128)(2,1)S(1)}, bf16[16,32,128]{2,1,0:T(8,128)(2,1)S(1)}, u32[]{:S(2)}, u32[]{:S(2)}) %collective-permute-start.5) | collective-permute-done | bytes 131104 | tf_op jit(solution)/shard_map/ppermute | solution.py:486
  33.8 0.0 collective-permute-done.6.refs_4_
  33.8 0.0 collective-permute-done.7.refs_5_
  33.8 0.0 collective-permute-done.8.refs_6_
  33.8 0.0 copy-done
  33.9 1.4 %peaks.1 = (f32[1,16]{1,0:T(1,128)}, f32[1,16]{1,0:T(1,128)}) custom-call(bf16[16,32,128]{2,1,0:T(8,128)(2,1)S(1)} %collective-permute-done.2.refs_0_, bf16[16,32,128]{2,1,0:T(8,128)(2,1)S(1)} %collective-permute-done.3.refs_1_, bf16[16,32,128]{2,1,0:T(8,128)(2,1)S(1)} %collective-permute-done.4.refs_2_, ...), custom_call_target="tpu_custom_call" | custom-call | tf_op jit(solution)/shard_map/peaks/pallas_call | solution.py:440
Async XLA Ops:
  3.8 2.7 %collective-permute-start.1 = (bf16[16,128,128]{2,1,0:T(8,128)(2,1)S(1)}, bf16[16,128,128]{2,1,0:T(8,128)(2,1)S(1)}, u32[]{:S(2)}, u32[]{:S(2)}) collective-permute-start(bf16[16,128,128]{2,1,0:T(8,128)(2,1)S(1)} %get-tuple-element.39), channel_id=1, source_target_pairs={{0,1},{1,0},{2,3},{3,2},{4,5},{5,4},{6,7},{7,6},{8,9},{9,8},{10,11... | collective-permute-start | bytes 1572872 | tf_op jit(solution)/shard_map/ppermute | solution.py:281
  5.1 2.0 %collective-permute-start = (bf16[16,128,128]{2,1,0:T(8,128)(2,1)S(1)}, bf16[16,128,128]{2,1,0:T(8,128)(2,1)S(1)}, u32[]{:S(2)}, u32[]{:S(2)}) collective-permute-start(bf16[16,128,128]{2,1,0:T(8,128)(2,1)S(1)} %get-tuple-element.38), channel_id=1, source_target_pairs={{0,1},{1,0},{2,3},{3,2},{4,5},{5,4},{6,7},{7,6},{8,9},{9,8},{10,11... | collective-permute-start | bytes 1572872 | tf_op jit(solution)/shard_map/ppermute | solution.py:285
  6.6 27.3 %copy-start = (f32[1,16]{1,0:T(1,128)S(1)}, f32[1,16]{1,0:T(1,128)}, u32[]{:S(2)}) copy-start(f32[1,16]{1,0:T(1,128)} %refs_9_.1) | copy-start | bytes 196
  7.4 10.2 %collective-permute-start.2 = (bf16[16,32,128]{2,1,0:T(8,128)(2,1)S(1)}, bf16[16,32,128]{2,1,0:T(8,128)(2,1)S(1)}, u32[]{:S(2)}, u32[]{:S(2)}) collective-permute-start(bf16[16,32,128]{2,1,0:T(8,128)(2,1)S(1)} %get-tuple-element.40), channel_id=1, source_target_pairs={{0,2},{2,0},{4,8},{6,10},{8,4},{10,6},{12,14},{14,12},{1,3},{3,1},... | collective-permute-start | bytes 393224 | tf_op jit(solution)/shard_map/ppermute | solution.py:486
  10.3 8.5 %collective-permute-start.3 = (bf16[16,32,128]{2,1,0:T(8,128)(2,1)S(1)}, bf16[16,32,128]{2,1,0:T(8,128)(2,1)S(1)}, u32[]{:S(2)}, u32[]{:S(2)}) collective-permute-start(bf16[16,32,128]{2,1,0:T(8,128)(2,1)S(1)} %get-tuple-element.41), channel_id=1, source_target_pairs={{0,4},{2,6},{4,0},{6,2},{8,12},{10,14},{12,8},{14,10},{1,5},{3,7},... | collective-permute-start | bytes 393224 | tf_op jit(solution)/shard_map/ppermute | solution.py:486
  11.9 15.8 %collective-permute-start.4 = (bf16[16,32,128]{2,1,0:T(8,128)(2,1)S(1)}, bf16[16,32,128]{2,1,0:T(8,128)(2,1)S(1)}, u32[]{:S(2)}, u32[]{:S(2)}) collective-permute-start(bf16[16,32,128]{2,1,0:T(8,128)(2,1)S(1)} %get-tuple-element.42), channel_id=1, source_target_pairs={{0,8},{2,10},{4,12},{6,14},{8,0},{10,2},{12,4},{14,6},{1,9},{3,11}... | collective-permute-start | bytes 393224 | tf_op jit(solution)/shard_map/ppermute | solution.py:486
  14.4 19.4 %collective-permute-start.5 = (bf16[16,32,128]{2,1,0:T(8,128)(2,1)S(1)}, bf16[16,32,128]{2,1,0:T(8,128)(2,1)S(1)}, u32[]{:S(2)}, u32[]{:S(2)}) collective-permute-start(bf16[16,32,128]{2,1,0:T(8,128)(2,1)S(1)} %get-tuple-element.43), channel_id=1, source_target_pairs={{0,10},{2,8},{4,14},{6,12},{8,2},{10,0},{12,6},{14,4},{1,11},{3,9}... | collective-permute-start | bytes 393224 | tf_op jit(solution)/shard_map/ppermute | solution.py:486
  15.7 18.1 %collective-permute-start.6 = (bf16[16,32,128]{2,1,0:T(8,128)(2,1)S(1)}, bf16[16,32,128]{2,1,0:T(8,128)(2,1)S(1)}, u32[]{:S(2)}, u32[]{:S(2)}) collective-permute-start(bf16[16,32,128]{2,1,0:T(8,128)(2,1)S(1)} %get-tuple-element.44), channel_id=1, source_target_pairs={{0,14},{2,12},{4,10},{6,8},{8,6},{10,4},{12,2},{14,0},{1,15},{3,13... | collective-permute-start | bytes 393224 | tf_op jit(solution)/shard_map/ppermute | solution.py:486
  17.7 16.2 %collective-permute-start.7 = (bf16[16,32,128]{2,1,0:T(8,128)(2,1)S(1)}, bf16[16,32,128]{2,1,0:T(8,128)(2,1)S(1)}, u32[]{:S(2)}, u32[]{:S(2)}) collective-permute-start(bf16[16,32,128]{2,1,0:T(8,128)(2,1)S(1)} %get-tuple-element.45), channel_id=1, source_target_pairs={{0,6},{2,4},{4,2},{6,0},{8,14},{10,12},{12,10},{14,8},{1,7},{3,5},... | collective-permute-start | bytes 393224 | tf_op jit(solution)/shard_map/ppermute | solution.py:486
  18.8 15.1 %collective-permute-start.8 = (bf16[16,32,128]{2,1,0:T(8,128)(2,1)S(1)}, bf16[16,32,128]{2,1,0:T(8,128)(2,1)S(1)}, u32[]{:S(2)}, u32[]{:S(2)}) collective-permute-start(bf16[16,32,128]{2,1,0:T(8,128)(2,1)S(1)} %get-tuple-element.46), channel_id=1, source_target_pairs={{0,12},{2,14},{4,6},{6,4},{8,10},{10,8},{12,0},{14,2},{1,13},{3,15... | collective-permute-start | bytes 393224 | tf_op jit(solution)/shard_map/ppermute | solution.py:486
